TPU v7x, 256 devices: a whole 4x4x8 slice. The times are simulated.
256 devices in a mesh: dp: 4 (over z_hi), dap: 64 (over y, x, z_lo, core).
Axes of the slice: x: 4, y: 4, z: 8 (z_hi: 4, z_lo: 2; z = z_hi * 2 + z_lo), core: 2. Of those that a mesh axis runs over, the one named last changes fastest.
Arguments:
- pair_state: bfloat16 [1024, 256, 128], P(('dp', 'dap')), parts along dimension 0, may hold values from -6 to 6
- cotangent: bfloat16 [1024, 256, 128], P(('dp', 'dap')), parts along dimension 0, may hold values from -6 to 6
- length: int32 [4], P('dp'), parts along dimension 0, may hold values from 128 to 256
- norm_gain: float32 [128], replicated, may hold values from 0.1 to 1.9
- norm_shift: float32 [128], replicated, may hold values from -3 to 3
- w_in: bfloat16 [128, 512], replicated, may hold values from -0.5 to 0.5
- w_bias: bfloat16 [128, 4], replicated, may hold values from -0.5 to 0.5
- w_out: bfloat16 [128, 128], replicated, may hold values from -0.5 to 0.5
Outputs:
- update: bfloat16 [1024, 256, 128], P(('dp', 'dap')), parts along dimension 0
- grad_pair: bfloat16 [1024, 256, 128], P(('dp', 'dap')), parts along dimension 0
- grad_w_in: float32 [512, 512], P('dp'), parts along dimension 0
- grad_w_out: float32 [512, 128], P('dp'), parts along dimension 0
- grad_w_bias: float32 [512, 4], P('dp'), parts along dimension 0
- grad_gain: float32 [512], P('dp'), parts along dimension 0
- grad_shift: float32 [512], P('dp'), parts along dimension 0
There are 4 independent parts, one for each index of `dp`. A program takes and returns all parts, laid end to end along the dimension named above; an argument that names none is the same for every part. Nothing has to cross between parts.
All inputs are finite; a program needn't handle non-finite values.
Results may differ from a plain program's by a relative error of at most 0.02.
Values may be sent and summed in bfloat16 or wider, within the bound.
A program may use at most 64 MiB of HBM per device.

v0:
```python
import math

import jax
import jax.numpy as jnp
from jax import lax
from jax.sharding import PartitionSpec as P

norm_epsilon = 1e-05
neg_fill = -1000000000.0


def layer_norm(pair_state, norm_gain, norm_shift):
    values = pair_state.astype(jnp.float32)
    row_mean = jnp.mean(values, -1, keepdims=True)
    centered = values - row_mean
    variance = jnp.mean(centered * centered, -1, keepdims=True)
    inv_std = lax.rsqrt(variance + norm_epsilon)
    normed = centered * inv_std
    return ((normed * norm_gain + norm_shift).astype(jnp.bfloat16), normed, inv_std)


def column_scores(q_col, k_col, bias_part, mask_part, score_scale):
    raw = jnp.einsum("ihd,khd->hik", q_col, k_col, preferred_element_type=jnp.float32)
    return raw * score_scale + bias_part.astype(jnp.float32) + mask_part


def attend_column(q_col, k_col, v_col, bias_all, mask_add, score_scale):
    scores = column_scores(q_col, k_col, bias_all, mask_add, score_scale)
    highest = jnp.max(scores, -1, keepdims=True)
    powers = jnp.exp(scores - highest)
    totals = jnp.sum(powers, -1)
    attended = jnp.einsum(
        "hik,khd->ihd", powers.astype(jnp.bfloat16), v_col, preferred_element_type=jnp.float32
    )
    attended = attended / jnp.transpose(totals)[:, :, None]
    return (attended, highest[..., 0] + jnp.log(totals))


def column_grads(
    q_col, k_col, v_col, bias_all, mask_add, score_scale, logsum, dout_heads, delta_sum
):
    scores = column_scores(q_col, k_col, bias_all, mask_add, score_scale)
    probs = jnp.exp(scores - logsum[:, :, None])
    probs_low = probs.astype(jnp.bfloat16)
    dvalue = jnp.einsum("hik,ihd->khd", probs_low, dout_heads, preferred_element_type=jnp.float32)
    dweights = jnp.einsum("ihd,khd->hik", dout_heads, v_col, preferred_element_type=jnp.float32)
    dscores = probs * (dweights - delta_sum[:, :, None])
    dscores_low = dscores.astype(jnp.bfloat16)
    dquery = (
        jnp.einsum("hik,khd->ihd", dscores_low, k_col, preferred_element_type=jnp.float32)
        * score_scale
    )
    key_grad = (
        jnp.einsum("hik,ihd->khd", dscores_low, q_col, preferred_element_type=jnp.float32)
        * score_scale
    )
    return (dquery, key_grad, dvalue, dscores)


def per_device(pair_state, cotangent, length, norm_gain, norm_shift, w_in, w_bias, w_out):
    head_count = w_bias.shape[1]
    inner = w_out.shape[0]
    head_width = inner // head_count
    score_scale = 1.0 / math.sqrt(head_width)
    normed_pair, normed, inv_std = layer_norm(pair_state, norm_gain, norm_shift)
    bias_rows = jnp.einsum(
        "kic,ch->hik", normed_pair, w_bias, preferred_element_type=jnp.float32
    ).astype(jnp.bfloat16)
    row_major = jnp.swapaxes(normed_pair, 0, 1)
    columns = lax.all_to_all(row_major, "dap", split_axis=0, concat_axis=1, tiled=True)
    local_cols = columns.shape[0]
    full_len = columns.shape[1]
    mask_add = jnp.where(jnp.arange(full_len) < length[0], 0.0, neg_fill).astype(jnp.float32)
    projected = jnp.einsum("jnc,cf->jnf", columns, w_in, preferred_element_type=jnp.float32)
    shape_heads = (local_cols, full_len, head_count, head_width)
    queries = projected[..., :inner].astype(jnp.bfloat16).reshape(shape_heads)
    keys_all = projected[..., inner : 2 * inner].astype(jnp.bfloat16).reshape(shape_heads)
    values_all = projected[..., 2 * inner : 3 * inner].astype(jnp.bfloat16).reshape(shape_heads)
    gate_vals = jax.nn.sigmoid(projected[..., 3 * inner :])
    bias_all = lax.all_gather(bias_rows, "dap", axis=2, tiled=True)

    def forward_column(items):
        q_col, k_col, v_col = items
        return attend_column(q_col, k_col, v_col, bias_all, mask_add, score_scale)

    attended, logsum = lax.map(forward_column, (queries, keys_all, values_all))
    attended_flat = attended.reshape(local_cols, full_len, inner)
    gated_out = (gate_vals * attended_flat).astype(jnp.bfloat16)
    out_cols = jnp.einsum(
        "jnf,fc->jnc", gated_out, w_out, preferred_element_type=jnp.float32
    ).astype(jnp.bfloat16)
    update = jnp.swapaxes(
        lax.all_to_all(out_cols, "dap", split_axis=1, concat_axis=0, tiled=True), 0, 1
    )
    cot_cols = lax.all_to_all(
        jnp.swapaxes(cotangent, 0, 1), "dap", split_axis=0, concat_axis=1, tiled=True
    )
    dgated = jnp.einsum("jnc,fc->jnf", cot_cols, w_out, preferred_element_type=jnp.float32)
    grad_out_part = jnp.einsum(
        "jnf,jnc->fc", gated_out, cot_cols, preferred_element_type=jnp.float32
    )
    dout_low = (dgated * gate_vals).astype(jnp.bfloat16)
    dgate_pre = dgated * attended_flat * gate_vals * (1.0 - gate_vals)
    delta_sum = jnp.swapaxes(
        jnp.sum((dout_low.astype(jnp.float32) * attended_flat).reshape(shape_heads), -1), 1, 2
    )
    dout_heads_all = dout_low.reshape(shape_heads)
    flat_shape = (local_cols, full_len, inner)

    def backward_column(bias_grad, items):
        q_col, k_col, v_col, lse_col, dout_col, delta_col = items
        dquery, key_grad, dvalue, dscores = column_grads(
            q_col, k_col, v_col, bias_all, mask_add, score_scale, lse_col, dout_col, delta_col
        )
        return (bias_grad + dscores, (dquery, key_grad, dvalue))

    start_grad = jnp.zeros((head_count, full_len, full_len), jnp.float32)
    bias_grad, grads_heads = lax.scan(
        backward_column,
        start_grad,
        (queries, keys_all, values_all, logsum, dout_heads_all, delta_sum),
    )
    dquery_all, key_grad_all, dvalue_all = grads_heads
    bias_share = lax.psum_scatter(bias_grad, "dap", scatter_dimension=2, tiled=True).astype(
        jnp.bfloat16
    )
    dprojected = jnp.concatenate(
        [
            dquery_all.reshape(flat_shape),
            key_grad_all.reshape(flat_shape),
            dvalue_all.reshape(flat_shape),
            dgate_pre,
        ],
        -1,
    ).astype(jnp.bfloat16)
    dcols = jnp.einsum("jnf,cf->jnc", dprojected, w_in, preferred_element_type=jnp.float32).astype(
        jnp.bfloat16
    )
    grad_in_part = jnp.einsum(
        "jnc,jnf->cf", columns, dprojected, preferred_element_type=jnp.float32
    )
    drows = jnp.swapaxes(
        lax.all_to_all(dcols, "dap", split_axis=1, concat_axis=0, tiled=True), 0, 1
    ).astype(jnp.float32)
    dnormed = drows + jnp.einsum(
        "hik,ch->kic", bias_share, w_bias, preferred_element_type=jnp.float32
    )
    grad_bias_part = jnp.einsum(
        "kic,hik->ch", normed_pair, bias_share, preferred_element_type=jnp.float32
    )
    scaled = dnormed * norm_gain
    grad_pair = (
        inv_std
        * (
            scaled
            - jnp.mean(scaled, -1, keepdims=True)
            - normed * jnp.mean(scaled * normed, -1, keepdims=True)
        )
    ).astype(jnp.bfloat16)
    grad_gain_part = jnp.sum(dnormed * normed, (0, 1))
    grad_shift_part = jnp.sum(dnormed, (0, 1))
    grad_w_in, grad_w_out, grad_w_bias, grad_gain, grad_shift = lax.psum(
        (grad_in_part, grad_out_part, grad_bias_part, grad_gain_part, grad_shift_part), "dap"
    )
    return (update, grad_pair, grad_w_in, grad_w_out, grad_w_bias, grad_gain, grad_shift)


def solution(mesh):
    return jax.shard_map(
        per_device,
        mesh=mesh,
        in_specs=(
            P(("dp", "dap"), None, None),
            P(("dp", "dap"), None, None),
            P("dp"),
            P(),
            P(),
            P(),
            P(),
            P(),
        ),
        out_specs=(
            P(("dp", "dap"), None, None),
            P(("dp", "dap"), None, None),
            P("dp", None),
            P("dp", None),
            P("dp", None),
            P("dp"),
            P("dp"),
        ),
        check_vma=False,
    )
```

profile of v0, /device:TPU:1, one launch (start us, length us, event | category | flops | bytes accessed | tf_op | source)
XLA Modules:
  0.0 1014.3 jit_solution(16076937248588887886)
XLA Ops:
  7.2 1.1 convert_reduce_fusion
  8.4 1.3 fusion.67
  9.7 1.3 fusion.80
  11.1 0.9 copy.64
  12.0 10.3 %all-to-all-start = ((bf16[256,4,128]{2,1,0:T(4,128)(2,1)}), bf16[256,4,128]{2,1,0:T(4,128)(2,1)S(1)}, u32[]{:S(2)}, u32[]{:S(2)}) async-start(bf16[256,4,128]{2,1,0:T(4,128)(2,1)} %copy.64), calls=%async_computation | async-start | bytes 524288 | tf_op jit(solution)/shard_map/all_to_all | solution.py:70
  22.8 84.7 %all_gather.3 = bf16[4,256,256]{1,0,2:T(4,128)(2,1)S(1)} all-gather(bf16[4,256,4]{1,0,2:T(4,128)(2,1)S(1)} %fusion.53), channel_id=1, replica_groups=mesh['dp'=4,'dap'=64] {'dap'}, dimensions={2}, use_global_device_ids=true | all-gather | bytes 532480 | tf_op jit(solution)/shard_map/all_gather | solution.py:80
  108.7 1.7 copy.113
  110.4 1.7 copy.114
  112.0 0.9 copy.95
  114.2 4.2 all-to-all-start.2
  118.5 1.8 fusion.90
  121.2 1.8 copy.66
  123.3 14.4 %while.32 = (s32[]{:T(128)}, f32[4,256,4,32]{1,3,2,0:T(8,128)}, f32[4,4,256]{2,1,0:T(4,128)}, bf16[4,256,4,32]{1,3,2,0:T(8,128)(2,1)}, bf16[4,256,4,32]{1,3,2,0:...) while((s32[]{:T(128)}, f32[4,256,4,32]{1,3,2,0:T(8,128)}, ...), condition=%wide.region_5.6_spmd.clone.clone, body=%wide.region_2.5_spmd.clone.sunk.clone | while | flops 35945984 | bytes 4035161 | solution.py:86
  125.1 1.8 fusion.137
  128.7 1.8 fusion.137
  132.3 1.8 fusion.137
  135.9 1.8 fusion.137
  137.7 1.2 copy.70
  139.0 2.4 convert_multiply_fusion
  142.3 1.8 copy.76
  144.1 24.3 %while.33 = (s32[]{:T(128)}, f32[4,256,256]{2,1,0:T(8,128)S(1)}, bf16[4,256,4,32]{1,3,2,0:T(8,128)(2,1)}, bf16[4,256,4,32]{1,3,2,0:T(8,128)(2,1)}, bf16[4,256,4,...) while((s32[]{:T(128)}, f32[4,256,256]{2,1,0:T(8,128)S(1)}, ...), condition=%wide.region_8.9_spmd.clone.clone, body=%wide.region_7.8_spmd.clone.sunk.clone | while | flops 86835712 | bytes 10321095 | solution.py:118
  146.0 1.5 select_add_fusion.3
  147.7 0.9 fusion.147
  148.6 1.7 fusion.149
  152.0 1.5 select_add_fusion.3
  154.6 1.7 fusion.149
  158.1 1.5 select_add_fusion.3
  159.8 0.9 fusion.147
  160.7 1.7 fusion.149
  164.2 1.5 select_add_fusion.3
  165.9 0.9 fusion.147
  166.8 1.6 fusion.149
  168.9 283.7 %all-reduce.7 = bf16[4,256,256]{1,0,2:T(4,128)(2,1)S(1)} all-reduce(f32[4,256,256]{1,0,2:T(4,128)S(1)} %copy.87), channel_id=2, replica_groups=mesh['dp'=4,'dap'=64] {'dap'}, use_global_device_ids=true, to_apply=%region_9.10.clone | all-reduce | flops 262144 | bytes 1572864
  452.5 1.1 copy.82
  453.8 1.1 copy.84
  455.5 0.9 copy.85
  456.4 10.6 %all-to-all-start.3 = ((bf16[4,256,128]{2,0,1:T(4,128)(2,1)}), bf16[4,256,128]{2,0,1:T(4,128)(2,1)S(1)}, u32[]{:S(2)}, u32[]{:S(2)}) async-start(bf16[4,256,128]{2,0,1:T(4,128)(2,1)} %copy.85), calls=%async_computation.3 | async-start | bytes 524288 | tf_op jit(solution)/shard_map/all_to_all | solution.py:143
  467.2 0.9 copy.71
  468.8 1.0 convolution_bitcast_fusion.2
  469.8 7.3 all-to-all-done.3
  477.0 4.5 all-to-all-start.1
  481.6 0.9 convolution_bitcast_fusion.3
  483.5 8.1 all-to-all-done.1
  492.6 138.8 %all-reduce.1 = (f32[128,4]{0,1:T(4,128)}, f32[128]{0:T(128)}, f32[128]{0:T(128)}) all-reduce(f32[128,4]{0,1:T(4,128)S(1)} %convolution_bitcast_fusion.4, f32[128]{0:T(128)S(1)} %get-tuple-element.253, f32[128]{0:T(128)S(1)} %reduce_sum.78), channel_id=1, replica_groups=mesh['dp'=4,'dap'=64] {'dap'}, use_global_device_ids=true, to_apply=%region_14.15 | all-reduce | flops 768 | bytes 6144 | tf_op jit(solution)/shard_map/psum | solution.py:162
  631.5 1.3 fusion.65
  632.8 371.5 %all-reduce.6.cloned.1.call-done = (f32[128,512]{1,0:T(8,128)}, f32[128,128]{1,0:T(8,128)}) async-done(((f32[128,512]{1,0:T(8,128)}, f32[128,128]{1,0:T(8,128)}), (f32[128,512]{1,0:T(8,128)}, f32[128,128]{1,0:T(8,128)})) %all-reduce.6.cloned.1.call-update) | async-done | bytes 327696 | tf_op jit(solution)/shard_map/psum | solution.py:162
  1004.3 1.7 copy.131
  1005.9 1.5 copy.132
  (114 shorter events, 24.6 us)
Async XLA Ops:
  7.2 111.3 %copy-start = (bf16[128,512]{1,0:T(8,128)(2,1)S(1)}, bf16[128,512]{1,0:T(8,128)(2,1)}, u32[]{:S(2)}) copy-start(bf16[128,512]{1,0:T(8,128)(2,1)} %param.17) | copy-start | bytes 393220
  7.2 15.2 %copy-start.1 = (bf16[4,256,128]{2,1,0:T(8,128)(2,1)S(1)}, bf16[4,256,128]{2,1,0:T(8,128)(2,1)}, u32[]{:S(2)}) copy-start(bf16[4,256,128]{2,1,0:T(8,128)(2,1)} %param.12) | copy-start | bytes 786436
  7.2 15.2 %copy-start.12 = (f32[128]{0:T(128)S(1)}, f32[128]{0:T(128)}, u32[]{:S(2)}) copy-start(f32[128]{0:T(128)} %param.15) | copy-start | bytes 1540
  7.2 15.2 %copy-start.15 = (f32[128]{0:T(128)S(1)}, f32[128]{0:T(128)}, u32[]{:S(2)}) copy-start(f32[128]{0:T(128)} %param.16) | copy-start | bytes 1540
  7.2 15.2 %copy-start.13 = (bf16[128,4]{0,1:T(4,128)(2,1)S(1)}, bf16[128,4]{0,1:T(4,128)(2,1)}, u32[]{:S(2)}) copy-start(bf16[128,4]{0,1:T(4,128)(2,1)} %param.18) | copy-start | bytes 3076
  12.0 102.2 %all-to-all-start = ((bf16[256,4,128]{2,1,0:T(4,128)(2,1)}), bf16[256,4,128]{2,1,0:T(4,128)(2,1)S(1)}, u32[]{:S(2)}, u32[]{:S(2)}) async-start(bf16[256,4,128]{2,1,0:T(4,128)(2,1)} %copy.64), calls=%async_computation | async-start | bytes 524288 | tf_op jit(solution)/shard_map/all_to_all | solution.py:70
  22.8 89.2 %copy-start.10 = (bf16[4,256,128]{2,1,0:T(8,128)(2,1)S(1)}, bf16[4,256,128]{2,1,0:T(8,128)(2,1)}, u32[]{:S(2)}) copy-start(bf16[4,256,128]{2,1,0:T(8,128)(2,1)} %param.13) | copy-start | bytes 786436
  107.5 5.4 copy-start.17
  114.2 24.8 %all-to-all-start.2 = ((bf16[256,4,128]{2,1,0:T(4,128)(2,1)}), bf16[256,4,128]{2,1,0:T(4,128)(2,1)S(1)}, u32[]{:S(2)}, u32[]{:S(2)}) async-start(bf16[256,4,128]{2,1,0:T(4,128)(2,1)} %bitcast.154), calls=%async_computation.2 | async-start | bytes 524288 | tf_op jit(solution)/shard_map/all_to_all | solution.py:95
  118.5 2.7 copy-start.2
  139.0 2.4 copy-start.4
  146.0 1.5 copy-start.7
  147.6 0.9 copy-start.8
  152.0 1.5 copy-start.7
  153.7 0.9 copy-start.8
  158.1 1.5 copy-start.7
  159.8 0.9 copy-start.8
  164.2 1.5 copy-start.7
  165.9 0.9 copy-start.8
  168.4 285.2 %copy-start.9 = (bf16[4,256,4,32]{1,3,2,0:T(8,128)(2,1)S(1)}, bf16[4,256,4,32]{1,3,2,0:T(8,128)(2,1)}, u32[]{:S(2)}) copy-start(bf16[4,256,4,32]{1,3,2,0:T(8,128)(2,1)} %get-tuple-element.123) | copy-start | bytes 786436
  168.8 286.1 %copy-start.18 = (bf16[4,256,128]{2,1,0:T(8,128)(2,1)S(1)}, bf16[4,256,128]{2,1,0:T(8,128)(2,1)}, u32[]{:S(2)}) copy-start(bf16[4,256,128]{2,1,0:T(8,128)(2,1)} %get-tuple-element.311) | copy-start | bytes 786436
  455.0 12.0 %copy-start.6 = (bf16[4,256,128]{2,1,0:T(8,128)(2,1)S(1)}, bf16[4,256,128]{2,1,0:T(8,128)(2,1)}, u32[]{:S(2)}) copy-start(bf16[4,256,128]{2,1,0:T(8,128)(2,1)} %get-tuple-element.312) | copy-start | bytes 786436
  455.0 12.0 %copy-start.11 = (bf16[128,128]{1,0:T(8,128)(2,1)S(1)}, bf16[128,128]{1,0:T(8,128)(2,1)}, u32[]{:S(2)}) copy-start(bf16[128,128]{1,0:T(8,128)(2,1)} %param.19) | copy-start | bytes 98308
  455.4 12.7 %copy-start.16 = (f32[128]{0:T(128)S(1)}, f32[128]{0:T(128)}, u32[]{:S(2)}) copy-start(f32[128]{0:T(128)} %param.16) | copy-start | bytes 1540
  455.5 13.3 %copy-start.3 = (bf16[64,4,4,128]{3,2,0,1:T(4,128)(2,1)S(1)}, bf16[64,4,4,128]{3,2,0,1:T(4,128)(2,1)}, u32[]{:S(2)}) copy-start(bf16[64,4,4,128]{3,2,0,1:T(4,128)(2,1)} %copy-done.2) | copy-start | bytes 786436
  456.4 20.7 %all-to-all-start.3 = ((bf16[4,256,128]{2,0,1:T(4,128)(2,1)}), bf16[4,256,128]{2,0,1:T(4,128)(2,1)S(1)}, u32[]{:S(2)}, u32[]{:S(2)}) async-start(bf16[4,256,128]{2,0,1:T(4,128)(2,1)} %copy.85), calls=%async_computation.3 | async-start | bytes 524288 | tf_op jit(solution)/shard_map/all_to_all | solution.py:143
  468.7 12.9 %copy-start.5 = (bf16[64,4,4,128]{3,2,0,1:T(4,128)(2,1)S(1)}, bf16[64,4,4,128]{3,2,0,1:T(4,128)(2,1)}, u32[]{:S(2)}) copy-start(bf16[64,4,4,128]{3,2,0,1:T(4,128)(2,1)} %copy-done.4) | copy-start | bytes 786436
  468.7 13.9 %copy-start.14 = (bf16[128,4]{0,1:T(4,128)(2,1)S(1)}, bf16[128,4]{0,1:T(4,128)(2,1)}, u32[]{:S(2)}) copy-start(bf16[128,4]{0,1:T(4,128)(2,1)} %param.18) | copy-start | bytes 3076
  477.0 14.6 %all-to-all-start.1 = ((bf16[4,256,128]{2,0,1:T(4,128)(2,1)}), bf16[4,256,128]{2,0,1:T(4,128)(2,1)S(1)}, u32[]{:S(2)}, u32[]{:S(2)}) async-start(bf16[4,256,128]{2,0,1:T(4,128)(2,1)} %copy.71), calls=%async_computation.1 | async-start | bytes 524288 | tf_op jit(solution)/shard_map/all_to_all | solution.py:93
  481.6 522.7 %all-reduce.6.cloned.1.call-start = ((), (), s32[]{:S(2)}) async-start(), calls=%async_computation.4 | async-start | bytes 655360 | tf_op jit(solution)/shard_map/psum | solution.py:162
Sparse Core Ops, SparseCore 0:
  485.7 518.5 all-reduce.5
where the time goes:
time: 1020 us; the launch traced here: 1010 us
  blocking collectives  507 us (50%)
  waiting for transfers between devices  387 us (38%)
  matrix products  36.1 us (4%)
  starting transfers between devices  29.7 us (3%)
  local copies, waits for them, and re-layouts  24 us (2%)
  between operations  15.1 us (1%)
  other arithmetic  15 us (1%)
    psum x1, waiting for transfers between devices, per_device(): lax.psum((grad_in_part, grad_out_part, grad_bias_part, grad_gain_part, gr...  372 us
    unnamed x1, blocking collectives  284 us
    psum x1, blocking collectives, per_device(): lax.psum((grad_in_part, grad_out_part, grad_bias_part, grad_gain_part, gr...  139 us
    all_gather x1, blocking collectives, per_device(): bias_all = lax.all_gather(bias_rows, 'dap', axis=2, tiled=True)  84.7 us
  transfers between devices with their start and end apart: 5, of which 3 were waited for; matrix products, arithmetic and copies ran while one was open for 3% of the time, Pallas kernels for 0%

commit v1 on v0

v1 whole, which is shorter than its diff:
```python
import functools
import math

import jax
import jax.numpy as jnp
from jax import lax
from jax.experimental import pallas as pl
from jax.experimental.pallas import tpu as pltpu
from jax.sharding import PartitionSpec as P

EPS = 1e-05
NEG = -1000000000.0
LOG2E = 1.4426950408889634
MESH = pl.DeviceIdType.MESH
F32 = jnp.float32
BF16 = jnp.bfloat16
ROWS = 4
COLS = 4
HEADS = 4
DIM = 32
N = 256
CH = 128


def nn(a, b):
    return lax.dot_general(a, b, (((1,), (0,)), ((), ())), preferred_element_type=F32)


def nt(a, b):
    return lax.dot_general(a, b, (((1,), (1,)), ((), ())), preferred_element_type=F32)


def tn(a, b):
    return lax.dot_general(a, b, (((0,), (0,)), ((), ())), preferred_element_type=F32)


def place(source_of):
    o = lax.broadcasted_iota(jnp.int32, (256, 256), 0)
    i = lax.broadcasted_iota(jnp.int32, (256, 256), 1)
    return jnp.where(source_of(o) == i, 1.0, 0.0).astype(BF16)


def rec_to_erc(o):
    return ((o >> 2) & 3) * 64 + ((o >> 4) << 2) + (o & 3)


def erc_to_cer(o):
    return ((o >> 2) & 15) * 16 + (o & 3) * 4 + (o >> 6)


def erc_to_rec(o):
    return ((o >> 2) & 15) * 16 + (o >> 6) * 4 + (o & 3)


def cer_to_erc(o):
    return (o & 3) * 64 + (o >> 4) * 4 + ((o >> 2) & 3)


def kernel(
    group,
    x_ref,
    cot_ref,
    len_ref,
    gain_ref,
    shift_ref,
    win_ref,
    wb_ref,
    wo_ref,
    upd_ref,
    gp_ref,
    gwin_ref,
    gwo_ref,
    gwb_ref,
    gg_ref,
    gs_ref,
    normed_ref,
    inv_ref,
    np_ref,
    pair_s,
    pair_r,
    cot_s,
    cot_r,
    bias_s,
    bias_r,
    cols_ref,
    cotc_ref,
    biasm_ref,
    proj_ref,
    gate_ref,
    dgate_ref,
    gated_ref,
    dproj_ref,
    bacc_ref,
    tmp_ref,
    upd_s,
    upd_r,
    dcol_s,
    dcol_r,
    bg_s,
    bg_r,
    par_f,
    par_s,
    par_r,
    sum_s,
    sum_r,
    small_s,
    small_r,
    send_sem,
    recv_sem,
):
    me = lax.axis_index("dap")

    def each_peer(body):
        def step(t, carry):
            body(lax.rem(me + t, group))
            return carry

        lax.fori_loop(1, group, step, 0)

    def send(which, source_of, dest):
        def one(e):
            pltpu.make_async_remote_copy(
                src_ref=source_of(e),
                dst_ref=dest.at[me],
                send_sem=send_sem.at[which],
                recv_sem=recv_sem.at[which],
                device_id={"dap": e},
                device_id_type=MESH,
            ).start()

        each_peer(one)

    def wait_recv(which, dest):
        part = dest.at[pl.ds(0, group - 1)]
        pltpu.make_async_copy(part, part, recv_sem.at[which]).wait()

    def wait_send(which, dest):
        part = dest.at[pl.ds(0, group - 1)]
        pltpu.make_async_copy(part, part, send_sem.at[which]).wait()

    barrier = pltpu.get_barrier_semaphore()
    each_peer(
        lambda e: pl.semaphore_signal(barrier, inc=1, device_id={"dap": e}, device_id_type=MESH)
    )

    rec_erc = place(rec_to_erc)
    erc_cer = place(erc_to_cer)
    erc_rec = place(erc_to_rec)
    cer_erc = place(cer_to_erc)

    for b in range(4):
        block = jnp.concatenate([cot_ref[r, 64 * b : 64 * b + 64, :] for r in range(ROWS)], 0)
        cot_s[16 * b : 16 * b + 16] = nn(rec_erc, block).astype(BF16).reshape(16, 16, CH)
    cot_r[me] = cot_s[me]

    pl.semaphore_wait(barrier, group - 1)
    send(0, lambda e: cot_s.at[e], cot_r)

    gain = gain_ref[...]
    shift = shift_ref[...]
    row_of = lax.broadcasted_iota(jnp.int32, (16, CH), 0)
    pick = jnp.where(
        (lax.broadcasted_iota(jnp.int32, (16, HEADS), 0) & 3)
        == lax.broadcasted_iota(jnp.int32, (16, HEADS), 1),
        1.0,
        0.0,
    ).astype(BF16)
    wb16 = nt(pick, wb_ref[...])
    wbr = [jnp.where((row_of >> 2) == r, wb16, 0.0).astype(BF16) for r in range(ROWS)]
    bias = jnp.zeros((16, N), F32)
    for r in range(ROWS):
        x = x_ref[r].astype(F32)
        mean = jnp.mean(x, -1, keepdims=True)
        cen = x - mean
        var = jnp.mean(cen * cen, -1, keepdims=True)
        inv = lax.rsqrt(var + EPS)
        normed = cen * inv
        normed_ref[r] = normed
        inv_ref[r] = jnp.broadcast_to(inv, (N, CH))
        low = (normed * gain + shift).astype(BF16)
        np_ref[r] = low
        bias += nt(wbr[r], low)
    for b in range(4):
        block = jnp.concatenate([np_ref[r, 64 * b : 64 * b + 64, :] for r in range(ROWS)], 0)
        pair_s[16 * b : 16 * b + 16] = nn(rec_erc, block).astype(BF16).reshape(16, 16, CH)
    bias_s[...] = bias.astype(BF16)
    pair_r[me] = pair_s[me]
    bias_r[me] = bias_s[...]
    send(1, lambda e: pair_s.at[e], pair_r)
    send(2, lambda e: bias_s, bias_r)

    w_in = win_ref[...]
    w_in_t = jnp.transpose(w_in.astype(F32)).astype(BF16)
    w_out = wo_ref[...]

    wait_recv(1, pair_r)
    for b in range(4):
        got = nn(erc_cer, pair_r[16 * b : 16 * b + 16].reshape(256, CH)).astype(BF16)
        for c in range(COLS):
            cols_ref[c, 64 * b : 64 * b + 64, :] = got[64 * c : 64 * c + 64]
    for j in range(COLS):
        projected = nt(w_in_t, cols_ref[j])
        proj_ref[j] = projected[: 3 * CH].astype(BF16)
        gate_ref[j] = jax.nn.sigmoid(projected[3 * CH :])

    wait_recv(0, cot_r)
    for b in range(4):
        got = nn(erc_cer, cot_r[16 * b : 16 * b + 16].reshape(256, CH)).astype(BF16)
        for c in range(COLS):
            cotc_ref[c, 64 * b : 64 * b + 64, :] = got[64 * c : 64 * c + 64]
    for j in range(COLS):
        dgate_ref[j] = nt(w_out, cotc_ref[j])

    wait_recv(2, bias_r)
    key = lax.broadcasted_iota(jnp.int32, (64, N), 0)
    for b in range(4):
        got = nn(erc_cer, bias_r[16 * b : 16 * b + 16].reshape(256, N)) * LOG2E
        mask = jnp.where(key + 64 * b < len_ref[0], 0.0, NEG)
        for h in range(HEADS):
            biasm_ref[h, 64 * b : 64 * b + 64, :] = got[64 * h : 64 * h + 64] + mask

    scale = 1.0 / math.sqrt(DIM)
    bacc_ref[...] = jnp.zeros_like(bacc_ref)

    def column(j, carry):
        for h in range(HEADS):
            rows = slice(DIM * h, DIM * h + DIM)
            q = proj_ref[j, DIM * h : DIM * h + DIM, :]
            k = proj_ref[j, CH + DIM * h : CH + DIM * h + DIM, :]
            v = proj_ref[j, 2 * CH + DIM * h : 2 * CH + DIM * h + DIM, :]
            s = tn(k, q) * (scale * LOG2E) + biasm_ref[h]
            p = jnp.exp2(s - jnp.max(s, 0, keepdims=True))
            inv_total = 1.0 / jnp.sum(p, 0, keepdims=True)
            p_low = p.astype(BF16)
            att = nn(v, p_low) * inv_total
            gate = gate_ref[j, rows, :]
            dgated = dgate_ref[j, rows, :]
            gated_ref[j, rows, :] = (gate * att).astype(BF16)
            datt = ((dgated * gate) * inv_total).astype(BF16)
            delta = jnp.sum(datt.astype(F32) * att, 0, keepdims=True)
            ds = p * (tn(v, datt) - delta)
            bacc_ref[h] += ds
            ds_low = ds.astype(BF16)
            dq = nn(k, ds_low) * scale
            dk = nt(q, ds_low) * scale
            dv = nt(datt, p_low)
            dg = dgated * att * gate * (1.0 - gate)
            dproj_ref[j, DIM * h : DIM * h + DIM, :] = dq.astype(BF16)
            dproj_ref[j, CH + DIM * h : CH + DIM * h + DIM, :] = dk.astype(BF16)
            dproj_ref[j, 2 * CH + DIM * h : 2 * CH + DIM * h + DIM, :] = dv.astype(BF16)
            dproj_ref[j, 3 * CH + DIM * h : 3 * CH + DIM * h + DIM, :] = dg.astype(BF16)
        return carry

    lax.fori_loop(0, COLS, column, 0)

    for b in range(4):
        block = jnp.concatenate([bacc_ref[h, 64 * b : 64 * b + 64, :] for h in range(HEADS)], 0)
        bg_s[16 * b : 16 * b + 16] = nn(cer_erc, block.astype(BF16)).astype(BF16).reshape(16, 16, N)
    bg_r[me] = bg_s[me]
    send(3, lambda e: bg_s.at[e], bg_r)

    for j in range(COLS):
        tmp_ref[j] = tn(dproj_ref[j], w_in_t).astype(BF16)
    for b in range(4):
        block = jnp.concatenate([tmp_ref[j, 64 * b : 64 * b + 64, :] for j in range(COLS)], 0)
        dcol_s[16 * b : 16 * b + 16] = nn(cer_erc, block).astype(BF16).reshape(16, 16, CH)
    dcol_r[me] = dcol_s[me]
    send(4, lambda e: dcol_s.at[e], dcol_r)

    for j in range(COLS):
        tmp_ref[j] = tn(gated_ref[j], w_out).astype(BF16)
    for b in range(4):
        block = jnp.concatenate([tmp_ref[j, 64 * b : 64 * b + 64, :] for j in range(COLS)], 0)
        upd_s[16 * b : 16 * b + 16] = nn(cer_erc, block).astype(BF16).reshape(16, 16, CH)
    upd_r[me] = upd_s[me]
    send(5, lambda e: upd_s.at[e], upd_r)

    g_in = nn(dproj_ref[0], cols_ref[0])
    g_out = nn(gated_ref[0], cotc_ref[0])
    for j in range(1, COLS):
        g_in += nn(dproj_ref[j], cols_ref[j])
        g_out += nn(gated_ref[j], cotc_ref[j])
    par_f[...] = jnp.zeros_like(par_f)
    for e in range(group):
        par_f[16 * e : 16 * e + 8, :] = g_in[8 * e : 8 * e + 8]
    par_f[pl.ds(8, group, stride=16), :] = g_out[:group]
    par_f[pl.ds(9, group, stride=16), :] = g_out[group:]
    par_s[...] = par_f[...].astype(BF16).reshape(group, 16, CH)
    par_r[me] = par_s[me]
    send(6, lambda e: par_s.at[e], par_r)

    wait_recv(3, bg_r)
    share = bg_r[0].astype(F32)
    for s in range(1, group):
        share += bg_r[s].astype(F32)
    share = share.astype(BF16)

    wait_recv(6, par_r)
    total = par_r[0].astype(F32)
    for s in range(1, group):
        total += par_r[s].astype(F32)
    sum_s[...] = total.astype(BF16)
    sum_r[me] = sum_s[...]
    send(7, lambda e: sum_s, sum_r)

    wait_recv(4, dcol_r)
    for b in range(4):
        got = nn(erc_rec, dcol_r[16 * b : 16 * b + 16].reshape(256, CH)).astype(BF16)
        for r in range(ROWS):
            tmp_ref[r, 64 * b : 64 * b + 64, :] = got[64 * r : 64 * r + 64]
    gwb = jnp.zeros((16, CH), F32)
    grad_gain = jnp.zeros((1, CH), F32)
    grad_shift = jnp.zeros((1, CH), F32)
    for r in range(ROWS):
        normed = normed_ref[r]
        dn = tmp_ref[r].astype(F32) + tn(share, wbr[r])
        gwb += jnp.where((row_of >> 2) == r, nn(share, np_ref[r]), 0.0)
        grad_gain += jnp.sum(dn * normed, 0, keepdims=True)
        grad_shift += jnp.sum(dn, 0, keepdims=True)
        scaled = dn * gain
        mean_s = jnp.mean(scaled, -1, keepdims=True)
        mean_sn = jnp.mean(scaled * normed, -1, keepdims=True)
        gp_ref[r] = (inv_ref[r] * (scaled - mean_s - normed * mean_sn)).astype(BF16)
    small_s[...] = jnp.zeros_like(small_s)
    small_s[0:4, :] = gwb[0:4] + gwb[4:8] + gwb[8:12] + gwb[12:16]
    small_s[4:5, :] = grad_gain
    small_s[5:6, :] = grad_shift
    small_r[me] = small_s[...]
    send(8, lambda e: small_s, small_r)

    wait_recv(5, upd_r)
    for b in range(4):
        got = nn(erc_rec, upd_r[16 * b : 16 * b + 16].reshape(256, CH)).astype(BF16)
        for r in range(ROWS):
            upd_ref[r, 64 * b : 64 * b + 64, :] = got[64 * r : 64 * r + 64]

    wait_recv(7, sum_r)
    par_f[...] = sum_r[...].astype(F32).reshape(group * 16, CH)
    gwo_ref[0:group, :] = par_f[pl.ds(8, group, stride=16), :]
    gwo_ref[group:, :] = par_f[pl.ds(9, group, stride=16), :]
    for q in range(4):
        part = jnp.concatenate(
            [par_f[16 * e : 16 * e + 8, :] for e in range(16 * q, 16 * q + 16)], 0
        )
        gwin_ref[:, CH * q : CH * q + CH] = jnp.transpose(part)

    wait_recv(8, small_r)
    small = small_r[0]
    for s in range(1, group):
        small += small_r[s]
    gwb_ref[...] = jnp.transpose(small)[:, 0:HEADS]
    gg_ref[...] = small[4:5]
    gs_ref[...] = small[5:6]

    for which, dest in enumerate(
        (cot_r, pair_r, bias_r, bg_r, dcol_r, upd_r, par_r, sum_r, small_r)
    ):
        wait_send(which, dest)


def per_device(group, pair_state, cotangent, length, norm_gain, norm_shift, w_in, w_bias, w_out):
    vmem = pl.BlockSpec(memory_space=pltpu.VMEM)
    smem = pl.BlockSpec(memory_space=pltpu.SMEM)
    block = (group, 16, CH)
    wide = (group, 16, N)
    out = pl.pallas_call(
        functools.partial(kernel, group),
        out_shape=(
            jax.ShapeDtypeStruct((ROWS, N, CH), BF16),
            jax.ShapeDtypeStruct((ROWS, N, CH), BF16),
            jax.ShapeDtypeStruct((CH, 4 * CH), F32),
            jax.ShapeDtypeStruct((CH, CH), F32),
            jax.ShapeDtypeStruct((CH, HEADS), F32),
            jax.ShapeDtypeStruct((1, CH), F32),
            jax.ShapeDtypeStruct((1, CH), F32),
        ),
        in_specs=[vmem, vmem, smem] + [vmem] * 5,
        out_specs=[vmem] * 7,
        scratch_shapes=[
            pltpu.VMEM((ROWS, N, CH), F32),
            pltpu.VMEM((ROWS, N, CH), F32),
            pltpu.VMEM((ROWS, N, CH), BF16),
            pltpu.VMEM(block, BF16),
            pltpu.VMEM(block, BF16),
            pltpu.VMEM(block, BF16),
            pltpu.VMEM(block, BF16),
            pltpu.VMEM((16, N), BF16),
            pltpu.VMEM(wide, BF16),
            pltpu.VMEM((COLS, N, CH), BF16),
            pltpu.VMEM((COLS, N, CH), BF16),
            pltpu.VMEM((HEADS, N, N), F32),
            pltpu.VMEM((COLS, 3 * CH, N), BF16),
            pltpu.VMEM((COLS, CH, N), F32),
            pltpu.VMEM((COLS, CH, N), F32),
            pltpu.VMEM((COLS, CH, N), BF16),
            pltpu.VMEM((COLS, 4 * CH, N), BF16),
            pltpu.VMEM((HEADS, N, N), F32),
            pltpu.VMEM((COLS, N, CH), BF16),
            pltpu.VMEM(block, BF16),
            pltpu.VMEM(block, BF16),
            pltpu.VMEM(block, BF16),
            pltpu.VMEM(block, BF16),
            pltpu.VMEM(wide, BF16),
            pltpu.VMEM(wide, BF16),
            pltpu.VMEM((group * 16, CH), F32),
            pltpu.VMEM(block, BF16),
            pltpu.VMEM(block, BF16),
            pltpu.VMEM((16, CH), BF16),
            pltpu.VMEM(block, BF16),
            pltpu.VMEM((8, CH), F32),
            pltpu.VMEM((group, 8, CH), F32),
            pltpu.SemaphoreType.DMA((9,)),
            pltpu.SemaphoreType.DMA((9,)),
        ],
        compiler_params=pltpu.CompilerParams(
            collective_id=0, has_side_effects=True, vmem_limit_bytes=40 * 2**20
        ),
    )(
        pair_state,
        cotangent,
        length,
        norm_gain.reshape(1, CH),
        norm_shift.reshape(1, CH),
        w_in,
        w_bias,
        w_out,
    )
    return (*out[:5], out[5].reshape(CH), out[6].reshape(CH))


def solution(mesh):
    split = P(("dp", "dap"), None, None)
    return jax.shard_map(
        functools.partial(per_device, mesh.shape["dap"]),
        mesh=mesh,
        in_specs=(split, split, P("dp"), P(), P(), P(), P(), P()),
        out_specs=(split, split, P("dp", None), P("dp", None), P("dp", None), P("dp"), P("dp")),
        check_vma=False,
    )
```

time: 1020 us -> 68.7 us (0.07)
  blocking collectives: 507 us -> 0 us
  waiting for transfers between devices: 387 us -> 0 us
  Pallas kernels: 0 us -> 59.1 us
  matrix products: 36.1 us -> 0 us
  starting transfers between devices: 29.7 us -> 0 us
  local copies, waits for them, and re-layouts: 24 us -> 8.04 us
  other arithmetic: 15 us -> 0 us
  between operations: 15.1 us -> 1.35 us
    psum x1 -> x0, waiting for transfers between devices: 372 us -> none  [per_device(): lax.psum((grad_in_part, grad_out_part, grad_bias_part, grad_gain_part, gr...]
    unnamed x1 -> x0, blocking collectives: 284 us -> none
    psum x1 -> x0, blocking collectives: 139 us -> none  [per_device(): lax.psum((grad_in_part, grad_out_part, grad_bias_part, grad_gain_part, gr...]
    all_gather x1 -> x0, blocking collectives: 84.7 us -> none  [per_device(): bias_all = lax.all_gather(bias_rows, 'dap', axis=2, tiled=True)]
    pallas_call x0 -> x1, Pallas kernels: none -> 59.1 us  [per_device(): pl.pallas_call(functools.partial(kernel, group), out_shape=(jax.ShapeDtyp...]
    dot_general x37 -> x0, matrix products: 36.1 us -> none  [the longest x4 7.04 us: attend_column(): jnp.einsum('hik,khd->ihd', powers.astype(jnp.bfloat16), v_col, preferred_...]
    all_to_all x4 -> x0, starting transfers between devices: 29.7 us -> none  [the longest x1 10.6 us: per_device(): lax.all_to_all(dcols, 'dap', split_axis=1, concat_axis=0, tiled=True)]
    all_to_all x4 -> x0, waiting for transfers between devices: 15.4 us -> none  [the longest x1 8.15 us: per_device(): lax.all_to_all(out_cols, 'dap', split_axis=1, concat_axis=0, tiled=True)]
  transfers between devices with their start and end apart: 5 -> 0, of which waited for: 3 -> 0; matrix products, arithmetic and copies ran while one was open for 3% -> 0% of each run, Pallas kernels for 0% -> 0%
where the time goes in v1:
time: 68.7 us; the launch traced here: 68.5 us
  Pallas kernels  59.1 us (86%)
  local copies, waits for them, and re-layouts  8.04 us (12%)
  between operations  1.35 us (2%)
    pallas_call x1, Pallas kernels, per_device(): pl.pallas_call(functools.partial(kernel, group), out_shape=(jax.ShapeDtyp...  59.1 us
    unnamed x20, local copies, waits for them, and re-layouts  8.04 us

profile of v1, /device:TPU:1, one launch (start us, length us, event | category | flops | bytes accessed | tf_op | source)
XLA Modules:
  0.0 68.5 jit_solution(11893268617121512074)
XLA Ops:
  0.6 0.0 copy-start.3
  1.3 0.0 copy-start.4
  1.3 0.0 copy-start.5
  1.3 0.8 %copy.15.wb_ref = bf16[128,4]{1,0:T(8,128)(2,1)S(1)} copy(bf16[128,4]{0,1:T(4,128)(2,1)} %param.14) | data formatting | bytes 2048 | tf_op args[6]
  2.1 0.0 copy-done.3
  2.1 0.0 copy-done.4
  2.1 0.0 copy-done.5
  2.2 0.0 copy-start
  2.2 0.9 %copy-done = bf16[4,256,128]{2,1,0:T(8,128)(2,1)S(1)} copy-done((bf16[4,256,128]{2,1,0:T(8,128)(2,1)S(1)}, bf16[4,256,128]{2,1,0:T(8,128)(2,1)}, u32[]{:S(2)}) %copy-start) | copy-done | bytes 262168
  3.1 0.0 copy-start.1
  3.1 0.9 %copy-done.1 = bf16[4,256,128]{2,1,0:T(8,128)(2,1)S(1)} copy-done((bf16[4,256,128]{2,1,0:T(8,128)(2,1)S(1)}, bf16[4,256,128]{2,1,0:T(8,128)(2,1)}, u32[]{:S(2)}) %copy-start.1) | copy-done | bytes 262168
  4.1 0.0 copy-start.2
  4.1 0.9 %copy-done.2 = bf16[128,512]{1,0:T(8,128)(2,1)S(1)} copy-done((bf16[128,512]{1,0:T(8,128)(2,1)S(1)}, bf16[128,512]{1,0:T(8,128)(2,1)}, u32[]{:S(2)}) %copy-start.2) | copy-done | bytes 131096
  5.0 59.1 %shard_map.135 = (bf16[4,256,128]{2,1,0:T(8,128)(2,1)S(1)}, bf16[4,256,128]{2,1,0:T(8,128)(2,1)S(1)}, f32[128,512]{1,0:T(8,128)S(1)}, f32[128,128]{1,0:T(8,128)S...) custom-call(bf16[4,256,128]{2,1,0:T(8,128)(2,1)S(1)} %copy-done, ...), custom_call_target="tpu_custom_call" | custom-call | tf_op jit(solution)/shard_map/pallas_call | solution.py:366
  64.1 0.7 copy.16
  64.7 0.7 %copy.24 = bf16[4,256,128]{2,1,0:T(8,128)(2,1)} copy(bf16[4,256,128]{2,1,0:T(8,128)(2,1)S(1)} %get-tuple-element.35) | data formatting | bytes 524288
  65.4 0.7 %copy.25 = bf16[4,256,128]{2,1,0:T(8,128)(2,1)} copy(bf16[4,256,128]{2,1,0:T(8,128)(2,1)S(1)} %get-tuple-element.36) | data formatting | bytes 524288
  66.1 0.7 %copy.26 = f32[128,512]{1,0:T(8,128)} copy(f32[128,512]{1,0:T(8,128)S(1)} %get-tuple-element.37) | data formatting | bytes 524288
  66.8 0.6 copy.27
  67.5 0.5 copy.28
  68.0 0.5 copy.29
Async XLA Ops:
  0.6 1.5 %copy-start.3 = (bf16[128,128]{1,0:T(8,128)(2,1)S(1)}, bf16[128,128]{1,0:T(8,128)(2,1)}, u32[]{:S(2)}) copy-start(bf16[128,128]{1,0:T(8,128)(2,1)} %wo_ref.1) | copy-start | bytes 98308
  1.3 0.8 %copy-start.4 = (f32[128]{0:T(128)S(1)}, f32[128]{0:T(128)}, u32[]{:S(2)}) copy-start(f32[128]{0:T(128)} %param.11) | copy-start | bytes 1540
  1.3 0.8 %copy-start.5 = (f32[128]{0:T(128)S(1)}, f32[128]{0:T(128)}, u32[]{:S(2)}) copy-start(f32[128]{0:T(128)} %param.12) | copy-start | bytes 1540
  2.2 1.0 %copy-start = (bf16[4,256,128]{2,1,0:T(8,128)(2,1)S(1)}, bf16[4,256,128]{2,1,0:T(8,128)(2,1)}, u32[]{:S(2)}) copy-start(bf16[4,256,128]{2,1,0:T(8,128)(2,1)} %x_ref.1) | copy-start | bytes 786436
  3.1 0.9 %copy-start.1 = (bf16[4,256,128]{2,1,0:T(8,128)(2,1)S(1)}, bf16[4,256,128]{2,1,0:T(8,128)(2,1)}, u32[]{:S(2)}) copy-start(bf16[4,256,128]{2,1,0:T(8,128)(2,1)} %cot_ref.1) | copy-start | bytes 786436
  4.1 0.9 %copy-start.2 = (bf16[128,512]{1,0:T(8,128)(2,1)S(1)}, bf16[128,512]{1,0:T(8,128)(2,1)}, u32[]{:S(2)}) copy-start(bf16[128,512]{1,0:T(8,128)(2,1)} %win_ref.1) | copy-start | bytes 393220

commit v2 on v1

v2 whole, which is shorter than its diff:
```python
import functools
import math

import jax
import jax.numpy as jnp
from jax import lax
from jax.experimental import pallas as pl
from jax.experimental.pallas import tpu as pltpu
from jax.sharding import PartitionSpec as P

EPS = 1e-05
NEG = -1000000000.0
LOG2E = 1.4426950408889634
MESH = pl.DeviceIdType.MESH
F32 = jnp.float32
BF16 = jnp.bfloat16
ROWS = 4
COLS = 4
HEADS = 4
DIM = 32
N = 256
CH = 128


def nn(a, b):
    return lax.dot_general(a, b, (((1,), (0,)), ((), ())), preferred_element_type=F32)


def nt(a, b):
    return lax.dot_general(a, b, (((1,), (1,)), ((), ())), preferred_element_type=F32)


def tn(a, b):
    return lax.dot_general(a, b, (((0,), (0,)), ((), ())), preferred_element_type=F32)


def place(source_of):
    o = lax.broadcasted_iota(jnp.int32, (256, 256), 0)
    i = lax.broadcasted_iota(jnp.int32, (256, 256), 1)
    return jnp.where(source_of(o) == i, 1.0, 0.0).astype(BF16)


def rec_to_erc(o):
    return ((o >> 2) & 3) * 64 + ((o >> 4) << 2) + (o & 3)


def erc_to_cer(o):
    return ((o >> 2) & 15) * 16 + (o & 3) * 4 + (o >> 6)


def erc_to_rec(o):
    return ((o >> 2) & 15) * 16 + (o >> 6) * 4 + (o & 3)


def cer_to_erc(o):
    return (o & 3) * 64 + (o >> 4) * 4 + ((o >> 2) & 3)


def kernel(
    group,
    x_hbm,
    cot_hbm,
    len_ref,
    gain_hbm,
    shift_hbm,
    win_hbm,
    wb_hbm,
    wo_hbm,
    upd_hbm,
    gp_hbm,
    gwin_hbm,
    gwo_hbm,
    gwb_hbm,
    gg_hbm,
    gs_hbm,
    upd_ref,
    gp_ref,
    gwin_ref,
    gwo_ref,
    gwb_ref,
    gg_ref,
    gs_ref,
    x_ref,
    cot_ref,
    gain_ref,
    shift_ref,
    win_ref,
    wb_ref,
    wo_ref,
    normed_ref,
    inv_ref,
    np_ref,
    pair_s,
    pair_r,
    cot_s,
    cot_r,
    bias_r,
    cols_ref,
    cotc_ref,
    biasm_ref,
    proj_ref,
    gate_ref,
    dgate_ref,
    gated_ref,
    att_ref,
    tot_ref,
    p_ref,
    dproj_ref,
    bacc_ref,
    tmp_ref,
    upd_s,
    upd_r,
    dcol_s,
    dcol_r,
    bg_s,
    bg_x,
    bg_t,
    bg_r,
    par_f,
    par_s,
    par_x,
    par_t,
    par_r,
    sum_r,
    small_s,
    small_r,
    in_sem,
    out_sem,
    send_sem,
    recv_sem,
):
    me = lax.axis_index("dap")
    core = lax.rem(me, 2)
    chip = lax.div(me, 2)
    twin = me + 1 - 2 * core
    chips = group // 2
    cot_x, pair_x, bias_x, bias_w, bg_w, bg_x_, dcol_x, upd_x, par_w, par_x_, sum_x, sum_w, small_x = range(13)

    loads = [
        pltpu.make_async_copy(src, dst, in_sem.at[n])
        for n, (src, dst) in enumerate(
            (
                (x_hbm, x_ref),
                (cot_hbm, cot_ref),
                (gain_hbm, gain_ref),
                (shift_hbm, shift_ref),
                (win_hbm, win_ref),
                (wb_hbm, wb_ref),
                (wo_hbm, wo_ref),
            )
        )
    ]
    for load in loads:
        load.start()

    stores = [
        pltpu.make_async_copy(src, dst, out_sem.at[n])
        for n, (src, dst) in enumerate(
            (
                (upd_ref, upd_hbm),
                (gp_ref, gp_hbm),
                (gwin_ref, gwin_hbm),
                (gwo_ref, gwo_hbm),
                (gwb_ref, gwb_hbm),
                (gg_ref, gg_hbm),
                (gs_ref, gs_hbm),
            )
        )
    ]

    def each_peer(body):
        def step(t, carry):
            body(lax.rem(me + t, group))
            return carry

        lax.fori_loop(1, group, step, 0)

    def each_chip(body):
        def step(t, carry):
            body(lax.rem(chip + t, chips))
            return carry

        lax.fori_loop(1, chips, step, 0)

    def copy(which, src, dst, device):
        return pltpu.make_async_remote_copy(
            src_ref=src,
            dst_ref=dst,
            send_sem=send_sem.at[which],
            recv_sem=recv_sem.at[which],
            device_id={"dap": device},
            device_id_type=MESH,
        )

    sent = []

    def send(which, source_of, dest):
        each_peer(lambda e: copy(which, source_of(e), dest.at[me], e).start())
        sent.append((which, dest.at[pl.ds(0, group - 1)]))

    def wait_recv(which, part):
        pltpu.make_async_copy(part, part, recv_sem.at[which]).wait()

    def wait_send(which, part):
        pltpu.make_async_copy(part, part, send_sem.at[which]).wait()

    barrier = pltpu.get_barrier_semaphore()
    each_peer(
        lambda e: pl.semaphore_signal(barrier, inc=1, device_id={"dap": e}, device_id_type=MESH)
    )

    rec_erc = place(rec_to_erc)
    erc_cer = place(erc_to_cer)
    erc_rec = place(erc_to_rec)
    cer_erc = place(cer_to_erc)
    row_of = lax.broadcasted_iota(jnp.int32, (16, CH), 0)
    pick = jnp.where(
        (lax.broadcasted_iota(jnp.int32, (16, HEADS), 0) & 3)
        == lax.broadcasted_iota(jnp.int32, (16, HEADS), 1),
        1.0,
        0.0,
    ).astype(BF16)

    for load in loads:
        load.wait()
    gain = gain_ref[...]
    shift = shift_ref[...]
    wb16 = nn(pick, wb_ref[...])
    wbr = [jnp.where((row_of >> 2) == r, wb16, 0.0).astype(BF16) for r in range(ROWS)]
    bias = jnp.zeros((16, N), F32)
    for r in range(ROWS):
        x = x_ref[r].astype(F32)
        mean = jnp.mean(x, -1, keepdims=True)
        cen = x - mean
        var = jnp.mean(cen * cen, -1, keepdims=True)
        inv = lax.rsqrt(var + EPS)
        normed = cen * inv
        normed_ref[r] = normed
        inv_ref[r] = jnp.broadcast_to(inv, (N, CH))
        low = (normed * gain + shift).astype(BF16)
        np_ref[r] = low
        bias += nt(wbr[r], low)
    for b in range(4):
        block = jnp.concatenate([np_ref[r, 64 * b : 64 * b + 64, :] for r in range(ROWS)], 0)
        pair_s[16 * b : 16 * b + 16] = nn(rec_erc, block).astype(BF16).reshape(16, 16, CH)
    for b in range(4):
        block = jnp.concatenate([cot_ref[r, 64 * b : 64 * b + 64, :] for r in range(ROWS)], 0)
        cot_s[16 * b : 16 * b + 16] = nn(rec_erc, block).astype(BF16).reshape(16, 16, CH)
    bias_r[chip, core] = bias.astype(BF16)
    pair_r[me] = pair_s[me]
    cot_r[me] = cot_s[me]

    pl.semaphore_wait(barrier, group - 1)

    def first(q):
        copy(pair_x, pair_s.at[2 * q + core], pair_r.at[me], 2 * q + core).start()
        copy(bias_x, bias_r.at[chip, core], bias_r.at[chip, core], 2 * q + core).start()
        copy(pair_x, pair_s.at[2 * q + 1 - core], pair_r.at[me], 2 * q + 1 - core).start()

    each_chip(first)
    copy(pair_x, pair_s.at[twin], pair_r.at[me], twin).start()
    sent.append((pair_x, pair_r.at[pl.ds(0, group - 1)]))
    sent.append((bias_x, bias_r.at[pl.ds(0, chips - 1), 0]))
    send(cot_x, lambda e: cot_s.at[e], cot_r)

    w_in = win_ref[...]
    w_in_t = jnp.transpose(w_in.astype(F32)).astype(BF16)
    w_out = wo_ref[...]

    wait_recv(pair_x, pair_r.at[pl.ds(0, group - 1)])
    for b in range(4):
        got = nn(erc_cer, pair_r[16 * b : 16 * b + 16].reshape(256, CH)).astype(BF16)
        for c in range(COLS):
            cols_ref[c, 64 * b : 64 * b + 64, :] = got[64 * c : 64 * c + 64]
    for j in range(COLS):
        projected = nt(w_in_t, cols_ref[j])
        proj_ref[j] = projected[: 3 * CH].astype(BF16)
        gate_ref[j] = jax.nn.sigmoid(projected[3 * CH :])

    wait_recv(bias_x, bias_r.at[pl.ds(0, chips - 1), 0])
    share = copy(bias_w, bias_r.at[:, core], bias_r.at[:, core], twin)
    share.start()
    share.wait()
    key = lax.broadcasted_iota(jnp.int32, (64, N), 0)
    for b in range(4):
        block = bias_r[8 * b : 8 * b + 8].reshape(256, N)
        got = nn(erc_cer, block) * LOG2E
        mask = jnp.where(key + 64 * b < len_ref[0], 0.0, NEG)
        for h in range(HEADS):
            biasm_ref[h, 64 * b : 64 * b + 64, :] = got[64 * h : 64 * h + 64] + mask

    scale = 1.0 / math.sqrt(DIM)

    def forward(j, carry):
        for h in range(HEADS):
            rows = slice(DIM * h, DIM * h + DIM)
            q = proj_ref[j, DIM * h : DIM * h + DIM, :]
            k = proj_ref[j, CH + DIM * h : CH + DIM * h + DIM, :]
            v = proj_ref[j, 2 * CH + DIM * h : 2 * CH + DIM * h + DIM, :]
            s = tn(k, q) * (scale * LOG2E) + biasm_ref[h]
            p = jnp.exp2(s - jnp.max(s, 0, keepdims=True))
            inv_total = 1.0 / jnp.sum(p, 0, keepdims=True)
            p_low = p.astype(BF16)
            p_ref[HEADS * j + h] = p_low
            att = nn(v, p_low) * inv_total
            att_ref[j, rows, :] = att
            tot_ref[j, h : h + 1, :] = inv_total
            gated_ref[j, rows, :] = (gate_ref[j, rows, :] * att).astype(BF16)
        return carry

    lax.fori_loop(0, COLS, forward, 0)

    for j in range(COLS):
        tmp_ref[j] = tn(gated_ref[j], w_out).astype(BF16)
    for b in range(4):
        block = jnp.concatenate([tmp_ref[j, 64 * b : 64 * b + 64, :] for j in range(COLS)], 0)
        upd_s[16 * b : 16 * b + 16] = nn(cer_erc, block).astype(BF16).reshape(16, 16, CH)
    upd_r[me] = upd_s[me]
    send(upd_x, lambda e: upd_s.at[e], upd_r)

    wait_recv(cot_x, cot_r.at[pl.ds(0, group - 1)])
    for b in range(4):
        got = nn(erc_cer, cot_r[16 * b : 16 * b + 16].reshape(256, CH)).astype(BF16)
        for c in range(COLS):
            cotc_ref[c, 64 * b : 64 * b + 64, :] = got[64 * c : 64 * c + 64]
    for j in range(COLS):
        dgate_ref[j] = nt(w_out, cotc_ref[j])

    bacc_ref[...] = jnp.zeros_like(bacc_ref)

    def backward(j, carry):
        for h in range(HEADS):
            rows = slice(DIM * h, DIM * h + DIM)
            q = proj_ref[j, DIM * h : DIM * h + DIM, :]
            k = proj_ref[j, CH + DIM * h : CH + DIM * h + DIM, :]
            v = proj_ref[j, 2 * CH + DIM * h : 2 * CH + DIM * h + DIM, :]
            att = att_ref[j, rows, :]
            gate = gate_ref[j, rows, :]
            dgated = dgate_ref[j, rows, :]
            datt = ((dgated * gate) * tot_ref[j, h : h + 1, :]).astype(BF16)
            delta = jnp.sum(datt.astype(F32) * att, 0, keepdims=True)
            p_low = p_ref[HEADS * j + h]
            ds = p_low.astype(F32) * (tn(v, datt) - delta)
            bacc_ref[h] += ds
            ds_low = ds.astype(BF16)
            dq = nn(k, ds_low) * scale
            dk = nt(q, ds_low) * scale
            dv = nt(datt, p_low)
            dg = dgated * att * gate * (1.0 - gate)
            dproj_ref[j, DIM * h : DIM * h + DIM, :] = dq.astype(BF16)
            dproj_ref[j, CH + DIM * h : CH + DIM * h + DIM, :] = dk.astype(BF16)
            dproj_ref[j, 2 * CH + DIM * h : 2 * CH + DIM * h + DIM, :] = dv.astype(BF16)
            dproj_ref[j, 3 * CH + DIM * h : 3 * CH + DIM * h + DIM, :] = dg.astype(BF16)
        return carry

    lax.fori_loop(0, COLS, backward, 0)

    for b in range(4):
        block = jnp.concatenate([bacc_ref[h, 64 * b : 64 * b + 64, :] for h in range(HEADS)], 0)
        got = nn(cer_erc, block.astype(BF16)).astype(BF16)
        bg_s[8 * b : 8 * b + 8] = got.reshape(8, 2, 16, N)
    bg_pass = copy(bg_w, bg_s.at[:, 1 - core], bg_x, twin)
    bg_pass.start()

    for j in range(COLS):
        tmp_ref[j] = tn(dproj_ref[j], w_in_t).astype(BF16)
    for b in range(4):
        block = jnp.concatenate([tmp_ref[j, 64 * b : 64 * b + 64, :] for j in range(COLS)], 0)
        dcol_s[16 * b : 16 * b + 16] = nn(cer_erc, block).astype(BF16).reshape(16, 16, CH)
    dcol_r[me] = dcol_s[me]
    send(dcol_x, lambda e: dcol_s.at[e], dcol_r)

    bg_pass.wait()
    for q in range(chips):
        bg_t[q] = (bg_s[q, core].astype(F32) + bg_x[q].astype(F32)).astype(BF16)
    bg_r[chip] = bg_t[chip]
    each_chip(lambda q: copy(bg_x_, bg_t.at[q], bg_r.at[chip], 2 * q + core).start())
    sent.append((bg_x_, bg_r.at[pl.ds(0, chips - 1)]))

    g_in = nn(dproj_ref[0], cols_ref[0])
    g_out = nn(gated_ref[0], cotc_ref[0])
    for j in range(1, COLS):
        g_in += nn(dproj_ref[j], cols_ref[j])
        g_out += nn(gated_ref[j], cotc_ref[j])
    par_f[...] = jnp.zeros_like(par_f)
    for e in range(group):
        par_f[16 * e : 16 * e + 8, :] = g_in[8 * e : 8 * e + 8]
    par_f[pl.ds(8, group, stride=16), :] = g_out[:group]
    par_f[pl.ds(9, group, stride=16), :] = g_out[group:]
    par_s[...] = par_f[...].astype(BF16).reshape(chips, 2, 16, CH)
    par_pass = copy(par_w, par_s.at[:, 1 - core], par_x, twin)
    par_pass.start()
    par_pass.wait()
    for q in range(chips):
        par_t[q] = (par_s[q, core].astype(F32) + par_x[q].astype(F32)).astype(BF16)
    par_r[chip] = par_t[chip]
    each_chip(lambda q: copy(par_x_, par_t.at[q], par_r.at[chip], 2 * q + core).start())
    sent.append((par_x_, par_r.at[pl.ds(0, chips - 1)]))

    wait_recv(bg_x_, bg_r.at[pl.ds(0, chips - 1)])
    bsum = bg_r[0].astype(F32)
    for s in range(1, chips):
        bsum += bg_r[s].astype(F32)
    bsum = bsum.astype(BF16)
    wait_recv(dcol_x, dcol_r.at[pl.ds(0, group - 1)])
    for b in range(4):
        got = nn(erc_rec, dcol_r[16 * b : 16 * b + 16].reshape(256, CH)).astype(BF16)
        for r in range(ROWS):
            tmp_ref[r, 64 * b : 64 * b + 64, :] = got[64 * r : 64 * r + 64]
    gwb = jnp.zeros((16, CH), F32)
    grad_gain = jnp.zeros((1, CH), F32)
    grad_shift = jnp.zeros((1, CH), F32)
    for r in range(ROWS):
        normed = normed_ref[r]
        dn = tmp_ref[r].astype(F32) + tn(bsum, wbr[r])
        att_ref[r, 0:CH, 0:CH] = dn[0:CH]
        att_ref[r, 0:CH, CH:] = dn[CH:]
        gwb += jnp.where((row_of >> 2) == r, nn(bsum, np_ref[r]), 0.0)
        grad_gain += jnp.sum(dn * normed, 0, keepdims=True)
        grad_shift += jnp.sum(dn, 0, keepdims=True)
    small_s[...] = jnp.zeros_like(small_s)
    small_s[0:4, :] = gwb[0:4] + gwb[4:8] + gwb[8:12] + gwb[12:16]
    small_s[4:5, :] = grad_gain
    small_s[5:6, :] = grad_shift
    small_r[me] = small_s[...]
    send(small_x, lambda e: small_s, small_r)

    wait_recv(par_x_, par_r.at[pl.ds(0, chips - 1)])
    total = par_r[0].astype(F32)
    for s in range(1, chips):
        total += par_r[s].astype(F32)
    sum_r[chip, core] = total.astype(BF16)
    each_chip(
        lambda q: copy(sum_x, sum_r.at[chip, core], sum_r.at[chip, core], 2 * q + core).start()
    )
    sent.append((sum_x, sum_r.at[pl.ds(0, chips - 1), 0]))

    for r in range(ROWS):
        normed = normed_ref[r]
        dn = jnp.concatenate([att_ref[r, 0:CH, 0:CH], att_ref[r, 0:CH, CH:]], 0)
        scaled = dn * gain
        mean_s = jnp.mean(scaled, -1, keepdims=True)
        mean_sn = jnp.mean(scaled * normed, -1, keepdims=True)
        gp_ref[r] = (inv_ref[r] * (scaled - mean_s - normed * mean_sn)).astype(BF16)

    stores[1].start()

    wait_recv(upd_x, upd_r.at[pl.ds(0, group - 1)])
    for b in range(4):
        got = nn(erc_rec, upd_r[16 * b : 16 * b + 16].reshape(256, CH)).astype(BF16)
        for r in range(ROWS):
            upd_ref[r, 64 * b : 64 * b + 64, :] = got[64 * r : 64 * r + 64]
    stores[0].start()

    wait_recv(sum_x, sum_r.at[pl.ds(0, chips - 1), 0])
    sum_pass = copy(sum_w, sum_r.at[:, core], sum_r.at[:, core], twin)
    sum_pass.start()

    wait_recv(small_x, small_r.at[pl.ds(0, group - 1)])
    small = small_r[0]
    for s in range(1, group):
        small += small_r[s]
    gwb_ref[...] = small[0:HEADS]
    gg_ref[...] = small[4:5]
    gs_ref[...] = small[5:6]
    for n in (4, 5, 6):
        stores[n].start()

    sum_pass.wait()
    par_f[...] = sum_r[...].astype(F32).reshape(group * 16, CH)
    gwo_ref[0:group, :] = par_f[pl.ds(8, group, stride=16), :]
    gwo_ref[group:, :] = par_f[pl.ds(9, group, stride=16), :]
    stores[3].start()
    for q in range(4):
        part = jnp.concatenate(
            [par_f[16 * e : 16 * e + 8, :] for e in range(16 * q, 16 * q + 16)], 0
        )
        gwin_ref[:, CH * q : CH * q + CH] = jnp.transpose(part)
    stores[2].start()

    for which, part in sent:
        wait_send(which, part)
    for store in stores:
        store.wait()


def finish(*refs):
    count = 7
    sources, results, held = refs[:count], refs[count : 2 * count], refs[2 * count : 3 * count]
    in_sem, out_sem = refs[3 * count :]
    loads = [pltpu.make_async_copy(sources[n], held[n], in_sem.at[n]) for n in range(count)]
    stores = [pltpu.make_async_copy(held[n], results[n], out_sem.at[n]) for n in range(count)]
    for load in loads:
        load.start()
    for load, store in zip(loads, stores):
        load.wait()
        store.start()
    for store in stores:
        store.wait()


def per_device(group, pair_state, cotangent, length, norm_gain, norm_shift, w_in, w_bias, w_out):
    vmem = pl.BlockSpec(memory_space=pltpu.VMEM)
    smem = pl.BlockSpec(memory_space=pltpu.SMEM)
    hbm = pl.BlockSpec(memory_space=pltpu.HBM)
    chips = group // 2
    block = (group, 16, CH)
    shapes = (
        jax.ShapeDtypeStruct((ROWS, N, CH), BF16),
        jax.ShapeDtypeStruct((ROWS, N, CH), BF16),
        jax.ShapeDtypeStruct((CH, 4 * CH), F32),
        jax.ShapeDtypeStruct((CH, CH), F32),
        jax.ShapeDtypeStruct((HEADS, CH), F32),
        jax.ShapeDtypeStruct((1, CH), F32),
        jax.ShapeDtypeStruct((1, CH), F32),
    )
    out = pl.pallas_call(
        functools.partial(kernel, group),
        out_shape=shapes,
        in_specs=[hbm, hbm, smem] + [hbm] * 5,
        out_specs=[hbm] * 7,
        scratch_shapes=[pltpu.VMEM(s.shape, s.dtype) for s in shapes]
        + [
            pltpu.VMEM((ROWS, N, CH), BF16),
            pltpu.VMEM((ROWS, N, CH), BF16),
            pltpu.VMEM((1, CH), F32),
            pltpu.VMEM((1, CH), F32),
            pltpu.VMEM((CH, 4 * CH), BF16),
            pltpu.VMEM((HEADS, CH), BF16),
            pltpu.VMEM((CH, CH), BF16),
            pltpu.VMEM((ROWS, N, CH), F32),
            pltpu.VMEM((ROWS, N, CH), F32),
            pltpu.VMEM((ROWS, N, CH), BF16),
            pltpu.VMEM(block, BF16),
            pltpu.VMEM(block, BF16),
            pltpu.VMEM(block, BF16),
            pltpu.VMEM(block, BF16),
            pltpu.VMEM((chips, 2, 16, N), BF16),
            pltpu.VMEM((COLS, N, CH), BF16),
            pltpu.VMEM((COLS, N, CH), BF16),
            pltpu.VMEM((HEADS, N, N), F32),
            pltpu.VMEM((COLS, 3 * CH, N), BF16),
            pltpu.VMEM((COLS, CH, N), F32),
            pltpu.VMEM((COLS, CH, N), F32),
            pltpu.VMEM((COLS, CH, N), BF16),
            pltpu.VMEM((COLS, CH, N), F32),
            pltpu.VMEM((COLS, 8, N), F32),
            pltpu.VMEM((COLS * HEADS, N, N), BF16),
            pltpu.VMEM((COLS, 4 * CH, N), BF16),
            pltpu.VMEM((HEADS, N, N), F32),
            pltpu.VMEM((COLS, N, CH), BF16),
            pltpu.VMEM(block, BF16),
            pltpu.VMEM(block, BF16),
            pltpu.VMEM(block, BF16),
            pltpu.VMEM(block, BF16),
            pltpu.VMEM((chips, 2, 16, N), BF16),
            pltpu.VMEM((chips, 16, N), BF16),
            pltpu.VMEM((chips, 16, N), BF16),
            pltpu.VMEM((chips, 16, N), BF16),
            pltpu.VMEM((group * 16, CH), F32),
            pltpu.VMEM((chips, 2, 16, CH), BF16),
            pltpu.VMEM((chips, 16, CH), BF16),
            pltpu.VMEM((chips, 16, CH), BF16),
            pltpu.VMEM((chips, 16, CH), BF16),
            pltpu.VMEM((chips, 2, 16, CH), BF16),
            pltpu.VMEM((8, CH), F32),
            pltpu.VMEM((group, 8, CH), F32),
            pltpu.SemaphoreType.DMA((7,)),
            pltpu.SemaphoreType.DMA((7,)),
            pltpu.SemaphoreType.DMA((13,)),
            pltpu.SemaphoreType.DMA((13,)),
        ],
        compiler_params=pltpu.CompilerParams(
            collective_id=0, has_side_effects=True, vmem_limit_bytes=60 * 2**20
        ),
    )(
        pair_state,
        cotangent,
        length,
        norm_gain.reshape(1, CH),
        norm_shift.reshape(1, CH),
        w_in,
        w_bias.T,
        w_out,
    )
    out = pl.pallas_call(
        finish,
        out_shape=shapes,
        in_specs=[hbm] * 7,
        out_specs=[hbm] * 7,
        scratch_shapes=[pltpu.VMEM(s.shape, s.dtype) for s in shapes]
        + [pltpu.SemaphoreType.DMA((7,)), pltpu.SemaphoreType.DMA((7,))],
        compiler_params=pltpu.CompilerParams(vmem_limit_bytes=60 * 2**20),
    )(*out)
    return (*out[:4], out[4].T, out[5].reshape(CH), out[6].reshape(CH))


def solution(mesh):
    split = P(("dp", "dap"), None, None)
    return jax.shard_map(
        functools.partial(per_device, mesh.shape["dap"]),
        mesh=mesh,
        in_specs=(split, split, P("dp"), P(), P(), P(), P(), P()),
        out_specs=(split, split, P("dp", None), P("dp", None), P("dp", None), P("dp"), P("dp")),
        check_vma=False,
    )
```

time: 68.7 us -> 57.2 us (0.83)
  local copies, waits for them, and re-layouts: 8.04 us -> 0 us
  Pallas kernels: 59.1 us -> 55.8 us
    unnamed x20 -> x0, local copies, waits for them, and re-layouts: 8.04 us -> none
    pallas_call x1 -> x2, Pallas kernels: 59.1 us -> 55.8 us  [the longest x1 53.8 us: per_device(): pl.pallas_call(functools.partial(kernel, group), out_shape=shapes, in_spe...]
where the time goes in v2:
time: 57.2 us; the launch traced here: 57.1 us
  Pallas kernels  55.8 us (98%)
  between operations  1.29 us (2%)
    pallas_call x1, Pallas kernels, per_device(): pl.pallas_call(functools.partial(kernel, group), out_shape=shapes, in_spe...  53.8 us
    pallas_call x1, Pallas kernels, per_device(): pl.pallas_call(finish, out_shape=shapes, in_specs=[hbm] * 7, out_specs=[h...  1.97 us

profile of v2, /device:TPU:1, one launch (start us, length us, event | category | flops | bytes accessed | tf_op | source)
XLA Modules:
  0.0 57.1 jit_solution(17221050707123420916)
XLA Ops:
  1.3 53.8 %shard_map.135 = (bf16[4,256,128]{2,1,0:T(8,128)(2,1)}, bf16[4,256,128]{2,1,0:T(8,128)(2,1)}, f32[128,512]{1,0:T(8,128)}, f32[128,128]{1,0:T(8,128)}, f32[4,128]...) custom-call(bf16[4,256,128]{2,1,0:T(8,128)(2,1)} %x_hbm.1, bf16[4,256,128]{2,1,0:T(8,128)(2,1)} %cot_hbm.1, ...), custom_call_target="tpu_custom_call" | custom-call | tf_op jit(solution)/shard_map/pallas_call | solution.py:517
  55.1 2.0 %shard_map.136 = (bf16[4,256,128]{2,1,0:T(8,128)(2,1)}, bf16[4,256,128]{2,1,0:T(8,128)(2,1)}, f32[128,512]{1,0:T(8,128)}, f32[128,128]{1,0:T(8,128)}, f32[4,128]...) custom-call(bf16[4,256,128]{2,1,0:T(8,128)(2,1)} %get-tuple-element.21.refs_0_, ...), custom_call_target="tpu_custom_call" | custom-call | tf_op jit(solution)/shard_map/pallas_call | solution.py:586

commit v3 on v2

--- a/solution.py
+++ b/solution.py
@@ -90,6 +90,9 @@
     normed_ref,
     inv_ref,
     np_ref,
+    high_ref,
+    low_ref,
+    dn_ref,
     pair_s,
     pair_r,
     cot_s,
@@ -116,6 +119,7 @@
     bg_x,
     bg_t,
     bg_r,
+    gin_ref,
     par_f,
     par_s,
     par_x,
@@ -134,7 +138,8 @@
     chip = lax.div(me, 2)
     twin = me + 1 - 2 * core
     chips = group // 2
-    cot_x, pair_x, bias_x, bias_w, bg_w, bg_x_, dcol_x, upd_x, par_w, par_x_, sum_x, sum_w, small_x = range(13)
+    cot_x, pair_x, bias_x, bias_w, bg_w, bg_x_, dcol_x, upd_x = 0, 1, 2, 3, 4, 6, 8, 9
+    par_w, par_x_, sum_x, sum_w, small_x = 10, 11, 12, 13, 14
 
     loads = [
         pltpu.make_async_copy(src, dst, in_sem.at[n])
@@ -168,19 +173,38 @@
         )
     ]
 
+    y_at = lax.div(chip, 8)
+    xs = [2 * lax.rem(lax.rem(lax.div(chip, 2), 4) + o, 4) for o in range(4)]
+    zs = [lax.rem(lax.rem(chip, 2) + o, 2) for o in range(2)]
+    around = [xs[x] + zs[z] for x in (2, 1, 3, 0) for z in (1, 0)]
+
+    def row_at(n):
+        return 8 * lax.rem(y_at + 2 - n + 3 * lax.div(n, 2) - 2 * lax.div(n, 3), 4)
+
+    def each_chip(body):
+        def step(n, carry):
+            for offset in around:
+                body(row_at(n) + offset)
+            return carry
+
+        lax.fori_loop(0, 3, step, 0)
+        for offset in around[:-1]:
+            body(8 * y_at + offset)
+
     def each_peer(body):
+        def both(q):
+            body(2 * q + 1 - core)
+            body(2 * q + core)
+
+        each_chip(both)
+        body(twin)
+
+    def near_peer(body):
         def step(t, carry):
             body(lax.rem(me + t, group))
             return carry
 
         lax.fori_loop(1, group, step, 0)
-
-    def each_chip(body):
-        def step(t, carry):
-            body(lax.rem(chip + t, chips))
-            return carry
-
-        lax.fori_loop(1, chips, step, 0)
 
     def copy(which, src, dst, device):
         return pltpu.make_async_remote_copy(
@@ -194,8 +218,8 @@
 
     sent = []
 
-    def send(which, source_of, dest):
-        each_peer(lambda e: copy(which, source_of(e), dest.at[me], e).start())
+    def send(which, source_of, dest, order=each_peer):
+        order(lambda e: copy(which, source_of(e), dest.at[me], e).start())
         sent.append((which, dest.at[pl.ds(0, group - 1)]))
 
     def wait_recv(which, part):
@@ -205,7 +229,7 @@
         pltpu.make_async_copy(part, part, send_sem.at[which]).wait()
 
     barrier = pltpu.get_barrier_semaphore()
-    each_peer(
+    near_peer(
         lambda e: pl.semaphore_signal(barrier, inc=1, device_id={"dap": e}, device_id_type=MESH)
     )
 
@@ -220,6 +244,24 @@
         1.0,
         0.0,
     ).astype(BF16)
+
+    source = lax.broadcasted_iota(jnp.int32, (256, CH), 0)
+    target = lax.broadcasted_iota(jnp.int32, (256, CH), 1)
+    pick_in = jnp.where(
+        (target >> 3) * 16 + (target & 7) == source, 1.0, 0.0
+    ).astype(BF16)
+    par_f[...] = jnp.zeros_like(par_f)
+    row = lax.broadcasted_iota(jnp.int32, (16, 16), 0)
+    col = lax.broadcasted_iota(jnp.int32, (16, 16), 1)
+    heads_at = [
+        [
+            jnp.where(
+                (((row & 3) >> 1) == pair) & ((row >> 2) * 4 + (row & 1) * 2 + half == col), 1.0, 0.0
+            ).astype(BF16)
+            for half in (0, 1)
+        ]
+        for pair in (0, 1)
+    ]
 
     for load in loads:
         load.wait()
@@ -239,6 +281,9 @@
         inv_ref[r] = jnp.broadcast_to(inv, (N, CH))
         low = (normed * gain + shift).astype(BF16)
         np_ref[r] = low
+        high = normed.astype(BF16)
+        high_ref[r] = high
+        low_ref[r] = (normed - high.astype(F32)).astype(BF16)
         bias += nt(wbr[r], low)
     for b in range(4):
         block = jnp.concatenate([np_ref[r, 64 * b : 64 * b + 64, :] for r in range(ROWS)], 0)
@@ -252,20 +297,22 @@
 
     pl.semaphore_wait(barrier, group - 1)
 
-    def first(q):
-        copy(pair_x, pair_s.at[2 * q + core], pair_r.at[me], 2 * q + core).start()
-        copy(bias_x, bias_r.at[chip, core], bias_r.at[chip, core], 2 * q + core).start()
-        copy(pair_x, pair_s.at[2 * q + 1 - core], pair_r.at[me], 2 * q + 1 - core).start()
-
-    each_chip(first)
-    copy(pair_x, pair_s.at[twin], pair_r.at[me], twin).start()
-    sent.append((pair_x, pair_r.at[pl.ds(0, group - 1)]))
+    each_chip(
+        lambda q: copy(
+            bias_x, bias_r.at[chip, core], bias_r.at[chip, core], 2 * q + core
+        ).start()
+    )
     sent.append((bias_x, bias_r.at[pl.ds(0, chips - 1), 0]))
+    send(pair_x, lambda e: pair_s.at[e], pair_r)
     send(cot_x, lambda e: cot_s.at[e], cot_r)
 
     w_in = win_ref[...]
     w_in_t = jnp.transpose(w_in.astype(F32)).astype(BF16)
     w_out = wo_ref[...]
+
+    wait_recv(bias_x, bias_r.at[pl.ds(0, chips - 1), 0])
+    share = copy(bias_w, bias_r.at[:, core], bias_r.at[:, core], twin)
+    share.start()
 
     wait_recv(pair_x, pair_r.at[pl.ds(0, group - 1)])
     for b in range(4):
@@ -277,9 +324,6 @@
         proj_ref[j] = projected[: 3 * CH].astype(BF16)
         gate_ref[j] = jax.nn.sigmoid(projected[3 * CH :])
 
-    wait_recv(bias_x, bias_r.at[pl.ds(0, chips - 1), 0])
-    share = copy(bias_w, bias_r.at[:, core], bias_r.at[:, core], twin)
-    share.start()
     share.wait()
     key = lax.broadcasted_iota(jnp.int32, (64, N), 0)
     for b in range(4):
@@ -310,26 +354,26 @@
 
     lax.fori_loop(0, COLS, forward, 0)
 
+    wait_recv(cot_x, cot_r.at[pl.ds(0, group - 1)])
     for j in range(COLS):
         tmp_ref[j] = tn(gated_ref[j], w_out).astype(BF16)
     for b in range(4):
         block = jnp.concatenate([tmp_ref[j, 64 * b : 64 * b + 64, :] for j in range(COLS)], 0)
         upd_s[16 * b : 16 * b + 16] = nn(cer_erc, block).astype(BF16).reshape(16, 16, CH)
-    upd_r[me] = upd_s[me]
-    send(upd_x, lambda e: upd_s.at[e], upd_r)
-
-    wait_recv(cot_x, cot_r.at[pl.ds(0, group - 1)])
-    for b in range(4):
         got = nn(erc_cer, cot_r[16 * b : 16 * b + 16].reshape(256, CH)).astype(BF16)
         for c in range(COLS):
             cotc_ref[c, 64 * b : 64 * b + 64, :] = got[64 * c : 64 * c + 64]
+    upd_r[me] = upd_s[me]
     for j in range(COLS):
         dgate_ref[j] = nt(w_out, cotc_ref[j])
 
     bacc_ref[...] = jnp.zeros_like(bacc_ref)
 
-    def backward(j, carry):
-        for h in range(HEADS):
+    def send_upd(e):
+        copy(upd_x, upd_s.at[e], upd_r.at[me], e).start()
+
+    def backward(j, heads):
+        for h in heads:
             rows = slice(DIM * h, DIM * h + DIM)
             q = proj_ref[j, DIM * h : DIM * h + DIM, :]
             k = proj_ref[j, CH + DIM * h : CH + DIM * h + DIM, :]
@@ -351,79 +395,113 @@
             dproj_ref[j, CH + DIM * h : CH + DIM * h + DIM, :] = dk.astype(BF16)
             dproj_ref[j, 2 * CH + DIM * h : 2 * CH + DIM * h + DIM, :] = dv.astype(BF16)
             dproj_ref[j, 3 * CH + DIM * h : 3 * CH + DIM * h + DIM, :] = dg.astype(BF16)
+
+    def gather_bias(pair):
+        for b in range(4):
+            block = jnp.concatenate(
+                [
+                    bacc_ref[h, 64 * b : 64 * b + 64, CH * half : CH * half + CH]
+                    for h in (2 * pair, 2 * pair + 1)
+                    for half in (0, 1)
+                ],
+                0,
+            )
+            got = nn(cer_erc, block.astype(BF16)).astype(BF16)
+            bg_s[pair, 8 * b : 8 * b + 8] = got.reshape(8, 2, 16, CH)
+        passing = copy(bg_w + pair, bg_s.at[pair, :, 1 - core], bg_x.at[pair], twin)
+        passing.start()
+        return passing
+
+    def send_bias(pair, passing):
+        passing.wait()
+        for q in range(chips):
+            bg_t[pair, q] = (
+                bg_s[pair, q, core].astype(F32) + bg_x[pair, q].astype(F32)
+            ).astype(BF16)
+        bg_r[pair, chip] = bg_t[pair, chip]
+        each_chip(
+            lambda q: copy(
+                bg_x_ + pair, bg_t.at[pair, q], bg_r.at[pair, chip], 2 * q + core
+            ).start()
+        )
+        sent.append((bg_x_ + pair, bg_r.at[pair, pl.ds(0, chips - 1)]))
+
+    def first_heads(j, carry):
+        for offset in around[:-1]:
+            send_upd(2 * (row_at(j) + offset) + 1 - core)
+            send_upd(2 * (row_at(j) + offset) + core)
+        backward(j, (0, 1))
         return carry
 
-    lax.fori_loop(0, COLS, backward, 0)
-
-    for b in range(4):
-        block = jnp.concatenate([bacc_ref[h, 64 * b : 64 * b + 64, :] for h in range(HEADS)], 0)
-        got = nn(cer_erc, block.astype(BF16)).astype(BF16)
-        bg_s[8 * b : 8 * b + 8] = got.reshape(8, 2, 16, N)
-    bg_pass = copy(bg_w, bg_s.at[:, 1 - core], bg_x, twin)
-    bg_pass.start()
-
-    for j in range(COLS):
-        tmp_ref[j] = tn(dproj_ref[j], w_in_t).astype(BF16)
+    lax.fori_loop(0, COLS, first_heads, 0)
+    for n in range(3):
+        send_upd(2 * (row_at(n) + around[-1]) + 1 - core)
+        send_upd(2 * (row_at(n) + around[-1]) + core)
+    send_upd(twin)
+    sent.append((upd_x, upd_r.at[pl.ds(0, group - 1)]))
+
+    passing = gather_bias(0)
+    g_out = nn(gated_ref[0], cotc_ref[0])
+    for j in range(1, COLS):
+        g_out += nn(gated_ref[j], cotc_ref[j])
+    par_f[pl.ds(8, group, stride=16), :] = g_out[:group]
+    par_f[pl.ds(9, group, stride=16), :] = g_out[group:]
+
+    def column_ends(j):
+        tmp_ref[j] = jnp.transpose(nn(w_in, dproj_ref[j])).astype(BF16)
+        g_in = nn(dproj_ref[j], cols_ref[j])
+        if j == 0:
+            gin_ref[...] = g_in
+        else:
+            gin_ref[...] += g_in
+
+    backward(0, (2, 3))
+    backward(1, (2, 3))
+    column_ends(0)
+    send_bias(0, passing)
+    backward(2, (2, 3))
+    column_ends(1)
+    backward(3, (2, 3))
+    column_ends(2)
+    passing = gather_bias(1)
+    column_ends(3)
+
     for b in range(4):
         block = jnp.concatenate([tmp_ref[j, 64 * b : 64 * b + 64, :] for j in range(COLS)], 0)
         dcol_s[16 * b : 16 * b + 16] = nn(cer_erc, block).astype(BF16).reshape(16, 16, CH)
     dcol_r[me] = dcol_s[me]
-    send(dcol_x, lambda e: dcol_s.at[e], dcol_r)
-
-    bg_pass.wait()
-    for q in range(chips):
-        bg_t[q] = (bg_s[q, core].astype(F32) + bg_x[q].astype(F32)).astype(BF16)
-    bg_r[chip] = bg_t[chip]
-    each_chip(lambda q: copy(bg_x_, bg_t.at[q], bg_r.at[chip], 2 * q + core).start())
-    sent.append((bg_x_, bg_r.at[pl.ds(0, chips - 1)]))
-
-    g_in = nn(dproj_ref[0], cols_ref[0])
-    g_out = nn(gated_ref[0], cotc_ref[0])
-    for j in range(1, COLS):
-        g_in += nn(dproj_ref[j], cols_ref[j])
-        g_out += nn(gated_ref[j], cotc_ref[j])
-    par_f[...] = jnp.zeros_like(par_f)
+
     for e in range(group):
-        par_f[16 * e : 16 * e + 8, :] = g_in[8 * e : 8 * e + 8]
-    par_f[pl.ds(8, group, stride=16), :] = g_out[:group]
-    par_f[pl.ds(9, group, stride=16), :] = g_out[group:]
+        par_f[16 * e : 16 * e + 8, :] = gin_ref[8 * e : 8 * e + 8, :]
     par_s[...] = par_f[...].astype(BF16).reshape(chips, 2, 16, CH)
     par_pass = copy(par_w, par_s.at[:, 1 - core], par_x, twin)
     par_pass.start()
+    send(dcol_x, lambda e: dcol_s.at[e], dcol_r)
     par_pass.wait()
     for q in range(chips):
         par_t[q] = (par_s[q, core].astype(F32) + par_x[q].astype(F32)).astype(BF16)
     par_r[chip] = par_t[chip]
     each_chip(lambda q: copy(par_x_, par_t.at[q], par_r.at[chip], 2 * q + core).start())
     sent.append((par_x_, par_r.at[pl.ds(0, chips - 1)]))
-
-    wait_recv(bg_x_, bg_r.at[pl.ds(0, chips - 1)])
-    bsum = bg_r[0].astype(F32)
-    for s in range(1, chips):
-        bsum += bg_r[s].astype(F32)
-    bsum = bsum.astype(BF16)
+    send_bias(1, passing)
+
+    wait_recv(upd_x, upd_r.at[pl.ds(0, group - 1)])
+    for b in range(4):
+        got = nn(erc_rec, upd_r[16 * b : 16 * b + 16].reshape(256, CH)).astype(BF16)
+        for r in range(ROWS):
+            upd_ref[r, 64 * b : 64 * b + 64, :] = got[64 * r : 64 * r + 64]
+    stores[0].start()
+
     wait_recv(dcol_x, dcol_r.at[pl.ds(0, group - 1)])
     for b in range(4):
-        got = nn(erc_rec, dcol_r[16 * b : 16 * b + 16].reshape(256, CH)).astype(BF16)
+        got = nn(erc_rec, dcol_r[16 * b : 16 * b + 16].reshape(256, CH))
         for r in range(ROWS):
-            tmp_ref[r, 64 * b : 64 * b + 64, :] = got[64 * r : 64 * r + 64]
-    gwb = jnp.zeros((16, CH), F32)
+            dn_ref[r, 64 * b : 64 * b + 64, :] = got[64 * r : 64 * r + 64]
     grad_gain = jnp.zeros((1, CH), F32)
     grad_shift = jnp.zeros((1, CH), F32)
     for r in range(ROWS):
-        normed = normed_ref[r]
-        dn = tmp_ref[r].astype(F32) + tn(bsum, wbr[r])
-        att_ref[r, 0:CH, 0:CH] = dn[0:CH]
-        att_ref[r, 0:CH, CH:] = dn[CH:]
-        gwb += jnp.where((row_of >> 2) == r, nn(bsum, np_ref[r]), 0.0)
-        grad_gain += jnp.sum(dn * normed, 0, keepdims=True)
-        grad_shift += jnp.sum(dn, 0, keepdims=True)
-    small_s[...] = jnp.zeros_like(small_s)
-    small_s[0:4, :] = gwb[0:4] + gwb[4:8] + gwb[8:12] + gwb[12:16]
-    small_s[4:5, :] = grad_gain
-    small_s[5:6, :] = grad_shift
-    small_r[me] = small_s[...]
-    send(small_x, lambda e: small_s, small_r)
+        grad_gain += jnp.sum(dn_ref[r] * normed_ref[r], 0, keepdims=True)
+        grad_shift += jnp.sum(dn_ref[r], 0, keepdims=True)
 
     wait_recv(par_x_, par_r.at[pl.ds(0, chips - 1)])
     total = par_r[0].astype(F32)
@@ -435,26 +513,50 @@
     )
     sent.append((sum_x, sum_r.at[pl.ds(0, chips - 1), 0]))
 
+    sums = []
+    for pair in range(2):
+        wait_recv(bg_x_ + pair, bg_r.at[pair, pl.ds(0, chips - 1)])
+        bsum = bg_r[pair, 0].astype(F32)
+        for s in range(1, chips):
+            bsum += bg_r[pair, s].astype(F32)
+        sums.append(bsum.astype(BF16))
+    bsum = jnp.concatenate(
+        [nn(heads_at[0][half], sums[0]) + nn(heads_at[1][half], sums[1]) for half in (0, 1)], 1
+    ).astype(BF16)
+    gwb = jnp.zeros((16, CH), F32)
+    part = jnp.zeros((16, CH), F32)
+    for r in range(ROWS):
+        here = (row_of >> 2) == r
+        gwb += jnp.where(here, nn(bsum, np_ref[r]), 0.0)
+        part += jnp.where(here, nn(bsum, high_ref[r]) + nn(bsum, low_ref[r]), 0.0)
+    grad_gain += jnp.sum(part * wb16, 0, keepdims=True)
+    grad_shift += jnp.sum(jnp.sum(bsum.astype(F32), 1, keepdims=True) * wb16, 0, keepdims=True)
+    small_s[0:4, :] = gwb[0:4] + gwb[4:8] + gwb[8:12] + gwb[12:16]
+    small_s[4:5, :] = grad_gain
+    small_s[5:6, :] = grad_shift
+    small_r[me] = small_s[...]
+    send(small_x, lambda e: small_s, small_r, near_peer)
+
     for r in range(ROWS):
         normed = normed_ref[r]
-        dn = jnp.concatenate([att_ref[r, 0:CH, 0:CH], att_ref[r, 0:CH, CH:]], 0)
-        scaled = dn * gain
+        scaled = (dn_ref[r] + tn(bsum, wbr[r])) * gain
         mean_s = jnp.mean(scaled, -1, keepdims=True)
         mean_sn = jnp.mean(scaled * normed, -1, keepdims=True)
         gp_ref[r] = (inv_ref[r] * (scaled - mean_s - normed * mean_sn)).astype(BF16)
-
     stores[1].start()
-
-    wait_recv(upd_x, upd_r.at[pl.ds(0, group - 1)])
-    for b in range(4):
-        got = nn(erc_rec, upd_r[16 * b : 16 * b + 16].reshape(256, CH)).astype(BF16)
-        for r in range(ROWS):
-            upd_ref[r, 64 * b : 64 * b + 64, :] = got[64 * r : 64 * r + 64]
-    stores[0].start()
 
     wait_recv(sum_x, sum_r.at[pl.ds(0, chips - 1), 0])
     sum_pass = copy(sum_w, sum_r.at[:, core], sum_r.at[:, core], twin)
     sum_pass.start()
+    sum_pass.wait()
+    for q in range(4):
+        rows = sum_r[8 * q : 8 * q + 8].reshape(256, CH)
+        gwin_ref[:, CH * q : CH * q + CH] = tn(rows, pick_in)
+    stores[2].start()
+    par_f[...] = sum_r[...].astype(F32).reshape(group * 16, CH)
+    gwo_ref[0:group, :] = par_f[pl.ds(8, group, stride=16), :]
+    gwo_ref[group:, :] = par_f[pl.ds(9, group, stride=16), :]
+    stores[3].start()
 
     wait_recv(small_x, small_r.at[pl.ds(0, group - 1)])
     small = small_r[0]
@@ -465,18 +567,6 @@
     gs_ref[...] = small[5:6]
     for n in (4, 5, 6):
         stores[n].start()
-
-    sum_pass.wait()
-    par_f[...] = sum_r[...].astype(F32).reshape(group * 16, CH)
-    gwo_ref[0:group, :] = par_f[pl.ds(8, group, stride=16), :]
-    gwo_ref[group:, :] = par_f[pl.ds(9, group, stride=16), :]
-    stores[3].start()
-    for q in range(4):
-        part = jnp.concatenate(
-            [par_f[16 * e : 16 * e + 8, :] for e in range(16 * q, 16 * q + 16)], 0
-        )
-        gwin_ref[:, CH * q : CH * q + CH] = jnp.transpose(part)
-    stores[2].start()
 
     for which, part in sent:
         wait_send(which, part)
@@ -531,6 +621,9 @@
             pltpu.VMEM((ROWS, N, CH), F32),
             pltpu.VMEM((ROWS, N, CH), F32),
             pltpu.VMEM((ROWS, N, CH), BF16),
+            pltpu.VMEM((ROWS, N, CH), BF16),
+            pltpu.VMEM((ROWS, N, CH), BF16),
+            pltpu.VMEM((ROWS, N, CH), F32),
             pltpu.VMEM(block, BF16),
             pltpu.VMEM(block, BF16),
             pltpu.VMEM(block, BF16),
@@ -553,22 +646,23 @@
             pltpu.VMEM(block, BF16),
             pltpu.VMEM(block, BF16),
             pltpu.VMEM(block, BF16),
-            pltpu.VMEM((chips, 2, 16, N), BF16),
-            pltpu.VMEM((chips, 16, N), BF16),
-            pltpu.VMEM((chips, 16, N), BF16),
-            pltpu.VMEM((chips, 16, N), BF16),
+            pltpu.VMEM((2, chips, 2, 16, CH), BF16),
+            pltpu.VMEM((2, chips, 16, CH), BF16),
+            pltpu.VMEM((2, chips, 16, CH), BF16),
+            pltpu.VMEM((2, chips, 16, CH), BF16),
+            pltpu.VMEM((4 * CH, CH), F32),
             pltpu.VMEM((group * 16, CH), F32),
             pltpu.VMEM((chips, 2, 16, CH), BF16),
             pltpu.VMEM((chips, 16, CH), BF16),
             pltpu.VMEM((chips, 16, CH), BF16),
             pltpu.VMEM((chips, 16, CH), BF16),
             pltpu.VMEM((chips, 2, 16, CH), BF16),
-            pltpu.VMEM((8, CH), F32),
-            pltpu.VMEM((group, 8, CH), F32),
+            pltpu.VMEM((6, CH), F32),
+            pltpu.VMEM((group, 6, CH), F32),
             pltpu.SemaphoreType.DMA((7,)),
             pltpu.SemaphoreType.DMA((7,)),
-            pltpu.SemaphoreType.DMA((13,)),
-            pltpu.SemaphoreType.DMA((13,)),
+            pltpu.SemaphoreType.DMA((15,)),
+            pltpu.SemaphoreType.DMA((15,)),
         ],
         compiler_params=pltpu.CompilerParams(
             collective_id=0, has_side_effects=True, vmem_limit_bytes=60 * 2**20

time: 57.2 us -> 51.3 us (0.90)
  Pallas kernels: 55.8 us -> 49.9 us
    pallas_call x1, Pallas kernels: 53.8 us -> 48 us  [per_device(): pl.pallas_call(functools.partial(kernel, group), out_shape=shapes, in_spe...]
where the time goes in v3:
time: 51.3 us; the launch traced here: 51.2 us
  Pallas kernels  49.9 us (97%)
  between operations  1.29 us (3%)
    pallas_call x1, Pallas kernels, per_device(): pl.pallas_call(functools.partial(kernel, group), out_shape=shapes, in_spe...  48 us
    pallas_call x1, Pallas kernels, per_device(): pl.pallas_call(finish, out_shape=shapes, in_specs=[hbm] * 7, out_specs=[h...  1.97 us

profile of v3, /device:TPU:1, one launch (start us, length us, event | category | flops | bytes accessed | tf_op | source)
XLA Modules:
  0.0 51.2 jit_solution(5293999292673192387)
XLA Ops:
  1.3 48.0 %shard_map.135 = (bf16[4,256,128]{2,1,0:T(8,128)(2,1)}, bf16[4,256,128]{2,1,0:T(8,128)(2,1)}, f32[128,512]{1,0:T(8,128)}, f32[128,128]{1,0:T(8,128)}, f32[4,128]...) custom-call(bf16[4,256,128]{2,1,0:T(8,128)(2,1)} %x_hbm.1, bf16[4,256,128]{2,1,0:T(8,128)(2,1)} %cot_hbm.1, ...), custom_call_target="tpu_custom_call" | custom-call | tf_op jit(solution)/shard_map/pallas_call | solution.py:607
  49.2 2.0 %shard_map.136 = (bf16[4,256,128]{2,1,0:T(8,128)(2,1)}, bf16[4,256,128]{2,1,0:T(8,128)(2,1)}, f32[128,512]{1,0:T(8,128)}, f32[128,128]{1,0:T(8,128)}, f32[4,128]...) custom-call(bf16[4,256,128]{2,1,0:T(8,128)(2,1)} %get-tuple-element.21.refs_0_, ...), custom_call_target="tpu_custom_call" | custom-call | tf_op jit(solution)/shard_map/pallas_call | solution.py:680

commit v4 on v3

--- a/solution.py
+++ b/solution.py
@@ -119,7 +119,10 @@
     bg_x,
     bg_t,
     bg_r,
-    gin_ref,
+    score_ref,
+    datt_ref,
+    delta_ref,
+    ds_ref,
     par_f,
     par_s,
     par_x,
@@ -179,12 +182,12 @@
     around = [xs[x] + zs[z] for x in (2, 1, 3, 0) for z in (1, 0)]
 
     def row_at(n):
-        return 8 * lax.rem(y_at + 2 - n + 3 * lax.div(n, 2) - 2 * lax.div(n, 3), 4)
+        return 8 * lax.rem(y_at + 2 - n + 3 * (n // 2) - 2 * (n // 3), 4)
 
     def each_chip(body):
         def step(n, carry):
             for offset in around:
-                body(row_at(n) + offset)
+                body(8 * lax.rem(y_at + 2 - n + 3 * lax.div(n, 2), 4) + offset)
             return carry
 
         lax.fori_loop(0, 3, step, 0)
@@ -335,24 +338,25 @@
 
     scale = 1.0 / math.sqrt(DIM)
 
-    def forward(j, carry):
-        for h in range(HEADS):
-            rows = slice(DIM * h, DIM * h + DIM)
-            q = proj_ref[j, DIM * h : DIM * h + DIM, :]
-            k = proj_ref[j, CH + DIM * h : CH + DIM * h + DIM, :]
-            v = proj_ref[j, 2 * CH + DIM * h : 2 * CH + DIM * h + DIM, :]
-            s = tn(k, q) * (scale * LOG2E) + biasm_ref[h]
-            p = jnp.exp2(s - jnp.max(s, 0, keepdims=True))
-            inv_total = 1.0 / jnp.sum(p, 0, keepdims=True)
-            p_low = p.astype(BF16)
-            p_ref[HEADS * j + h] = p_low
-            att = nn(v, p_low) * inv_total
-            att_ref[j, rows, :] = att
-            tot_ref[j, h : h + 1, :] = inv_total
-            gated_ref[j, rows, :] = (gate_ref[j, rows, :] * att).astype(BF16)
-        return carry
-
-    lax.fori_loop(0, COLS, forward, 0)
+    units = [(j, h) for j in range(COLS) for h in range(HEADS)]
+
+    def part_of(which, j, h):
+        first = CH * which + DIM * h
+        return proj_ref[j, first : first + DIM, :]
+
+    for j, h in units:
+        raw = tn(part_of(1, j, h), part_of(0, j, h))
+        score_ref[HEADS * j + h] = raw * (scale * LOG2E) + biasm_ref[h]
+    for j, h in units:
+        score = score_ref[HEADS * j + h]
+        p = jnp.exp2(score - jnp.max(score, 0, keepdims=True))
+        tot_ref[j, h : h + 1, :] = 1.0 / jnp.sum(p, 0, keepdims=True)
+        p_ref[HEADS * j + h] = p.astype(BF16)
+    for j, h in units:
+        rows = slice(DIM * h, DIM * h + DIM)
+        att = nn(part_of(2, j, h), p_ref[HEADS * j + h]) * tot_ref[j, h : h + 1, :]
+        att_ref[j, rows, :] = att
+        gated_ref[j, rows, :] = (gate_ref[j, rows, :] * att).astype(BF16)
 
     wait_recv(cot_x, cot_r.at[pl.ds(0, group - 1)])
     for j in range(COLS):
@@ -367,34 +371,47 @@
     for j in range(COLS):
         dgate_ref[j] = nt(w_out, cotc_ref[j])
 
-    bacc_ref[...] = jnp.zeros_like(bacc_ref)
-
     def send_upd(e):
         copy(upd_x, upd_s.at[e], upd_r.at[me], e).start()
 
-    def backward(j, heads):
+    def score_grads(heads):
+        for j in range(COLS):
+            for h in heads:
+                rows = slice(DIM * h, DIM * h + DIM)
+                att = att_ref[j, rows, :]
+                gate = gate_ref[j, rows, :]
+                dgated = dgate_ref[j, rows, :]
+                datt = ((dgated * gate) * tot_ref[j, h : h + 1, :]).astype(BF16)
+                datt_ref[j, rows, :] = datt
+                delta_ref[j, h : h + 1, :] = jnp.sum(datt.astype(F32) * att, 0, keepdims=True)
+                dg = dgated * att * gate * (1.0 - gate)
+                dproj_ref[j, 3 * CH + DIM * h : 3 * CH + DIM * h + DIM, :] = dg.astype(BF16)
         for h in heads:
-            rows = slice(DIM * h, DIM * h + DIM)
-            q = proj_ref[j, DIM * h : DIM * h + DIM, :]
-            k = proj_ref[j, CH + DIM * h : CH + DIM * h + DIM, :]
-            v = proj_ref[j, 2 * CH + DIM * h : 2 * CH + DIM * h + DIM, :]
-            att = att_ref[j, rows, :]
-            gate = gate_ref[j, rows, :]
-            dgated = dgate_ref[j, rows, :]
-            datt = ((dgated * gate) * tot_ref[j, h : h + 1, :]).astype(BF16)
-            delta = jnp.sum(datt.astype(F32) * att, 0, keepdims=True)
-            p_low = p_ref[HEADS * j + h]
-            ds = p_low.astype(F32) * (tn(v, datt) - delta)
-            bacc_ref[h] += ds
-            ds_low = ds.astype(BF16)
-            dq = nn(k, ds_low) * scale
-            dk = nt(q, ds_low) * scale
-            dv = nt(datt, p_low)
-            dg = dgated * att * gate * (1.0 - gate)
-            dproj_ref[j, DIM * h : DIM * h + DIM, :] = dq.astype(BF16)
-            dproj_ref[j, CH + DIM * h : CH + DIM * h + DIM, :] = dk.astype(BF16)
-            dproj_ref[j, 2 * CH + DIM * h : 2 * CH + DIM * h + DIM, :] = dv.astype(BF16)
-            dproj_ref[j, 3 * CH + DIM * h : 3 * CH + DIM * h + DIM, :] = dg.astype(BF16)
+            for j in range(COLS):
+                rows = slice(DIM * h, DIM * h + DIM)
+                dweights = tn(part_of(2, j, h), datt_ref[j, rows, :])
+                p = p_ref[HEADS * j + h].astype(F32)
+                ds = p * (dweights - delta_ref[j, h : h + 1, :])
+                if j == 0:
+                    bacc_ref[h] = ds
+                else:
+                    bacc_ref[h] += ds
+                ds_ref[HEADS * j + h] = ds.astype(BF16)
+
+    def input_grads(heads):
+        for which in range(3):
+            for j in range(COLS):
+                for h in heads:
+                    ds = ds_ref[HEADS * j + h]
+                    if which == 0:
+                        grad = nn(part_of(1, j, h), ds) * scale
+                    elif which == 1:
+                        grad = nt(part_of(0, j, h), ds) * scale
+                    else:
+                        rows = slice(DIM * h, DIM * h + DIM)
+                        grad = nt(datt_ref[j, rows, :], p_ref[HEADS * j + h])
+                    first = CH * which + DIM * h
+                    dproj_ref[j, first : first + DIM, :] = grad.astype(BF16)
 
     def gather_bias(pair):
         for b in range(4):
@@ -426,45 +443,34 @@
         )
         sent.append((bg_x_ + pair, bg_r.at[pair, pl.ds(0, chips - 1)]))
 
-    def first_heads(j, carry):
+    for j in range(COLS):
         for offset in around[:-1]:
             send_upd(2 * (row_at(j) + offset) + 1 - core)
             send_upd(2 * (row_at(j) + offset) + core)
-        backward(j, (0, 1))
-        return carry
-
-    lax.fori_loop(0, COLS, first_heads, 0)
     for n in range(3):
         send_upd(2 * (row_at(n) + around[-1]) + 1 - core)
         send_upd(2 * (row_at(n) + around[-1]) + core)
     send_upd(twin)
     sent.append((upd_x, upd_r.at[pl.ds(0, group - 1)]))
 
-    passing = gather_bias(0)
+    score_grads((0, 1))
+    first_pass = gather_bias(0)
+    score_grads((2, 3))
+    second_pass = gather_bias(1)
+    input_grads((0, 1))
+    send_bias(0, first_pass)
+    send_bias(1, second_pass)
+    input_grads((2, 3))
+
     g_out = nn(gated_ref[0], cotc_ref[0])
+    g_in = nn(dproj_ref[0], cols_ref[0])
     for j in range(1, COLS):
         g_out += nn(gated_ref[j], cotc_ref[j])
+        g_in += nn(dproj_ref[j], cols_ref[j])
     par_f[pl.ds(8, group, stride=16), :] = g_out[:group]
     par_f[pl.ds(9, group, stride=16), :] = g_out[group:]
-
-    def column_ends(j):
+    for j in range(COLS):
         tmp_ref[j] = jnp.transpose(nn(w_in, dproj_ref[j])).astype(BF16)
-        g_in = nn(dproj_ref[j], cols_ref[j])
-        if j == 0:
-            gin_ref[...] = g_in
-        else:
-            gin_ref[...] += g_in
-
-    backward(0, (2, 3))
-    backward(1, (2, 3))
-    column_ends(0)
-    send_bias(0, passing)
-    backward(2, (2, 3))
-    column_ends(1)
-    backward(3, (2, 3))
-    column_ends(2)
-    passing = gather_bias(1)
-    column_ends(3)
 
     for b in range(4):
         block = jnp.concatenate([tmp_ref[j, 64 * b : 64 * b + 64, :] for j in range(COLS)], 0)
@@ -472,7 +478,7 @@
     dcol_r[me] = dcol_s[me]
 
     for e in range(group):
-        par_f[16 * e : 16 * e + 8, :] = gin_ref[8 * e : 8 * e + 8, :]
+        par_f[16 * e : 16 * e + 8, :] = g_in[8 * e : 8 * e + 8]
     par_s[...] = par_f[...].astype(BF16).reshape(chips, 2, 16, CH)
     par_pass = copy(par_w, par_s.at[:, 1 - core], par_x, twin)
     par_pass.start()
@@ -483,7 +489,6 @@
     par_r[chip] = par_t[chip]
     each_chip(lambda q: copy(par_x_, par_t.at[q], par_r.at[chip], 2 * q + core).start())
     sent.append((par_x_, par_r.at[pl.ds(0, chips - 1)]))
-    send_bias(1, passing)
 
     wait_recv(upd_x, upd_r.at[pl.ds(0, group - 1)])
     for b in range(4):
@@ -650,7 +655,10 @@
             pltpu.VMEM((2, chips, 16, CH), BF16),
             pltpu.VMEM((2, chips, 16, CH), BF16),
             pltpu.VMEM((2, chips, 16, CH), BF16),
-            pltpu.VMEM((4 * CH, CH), F32),
+            pltpu.VMEM((COLS * HEADS, N, N), F32),
+            pltpu.VMEM((COLS, CH, N), BF16),
+            pltpu.VMEM((COLS, 8, N), F32),
+            pltpu.VMEM((COLS * HEADS, N, N), BF16),
             pltpu.VMEM((group * 16, CH), F32),
             pltpu.VMEM((chips, 2, 16, CH), BF16),
             pltpu.VMEM((chips, 16, CH), BF16),

time: 51.3 us -> 46.3 us (0.903)
  Pallas kernels: 49.9 us -> 44.9 us
    pallas_call x1, Pallas kernels: 48 us -> 43 us  [per_device(): pl.pallas_call(functools.partial(kernel, group), out_shape=shapes, in_spe...]
where the time goes in v4:
time: 46.3 us; the launch traced here: 46.2 us
  Pallas kernels  44.9 us (97%)
  between operations  1.29 us (3%)
    pallas_call x1, Pallas kernels, per_device(): pl.pallas_call(functools.partial(kernel, group), out_shape=shapes, in_spe...  43 us
    pallas_call x1, Pallas kernels, per_device(): pl.pallas_call(finish, out_shape=shapes, in_specs=[hbm] * 7, out_specs=[h...  1.97 us

profile of v4, /device:TPU:1, one launch (start us, length us, event | category | flops | bytes accessed | tf_op | source)
XLA Modules:
  0.0 46.2 jit_solution(6096596371879648689)
XLA Ops:
  1.3 43.0 %shard_map.135 = (bf16[4,256,128]{2,1,0:T(8,128)(2,1)}, bf16[4,256,128]{2,1,0:T(8,128)(2,1)}, f32[128,512]{1,0:T(8,128)}, f32[128,128]{1,0:T(8,128)}, f32[4,128]...) custom-call(bf16[4,256,128]{2,1,0:T(8,128)(2,1)} %x_hbm.1, bf16[4,256,128]{2,1,0:T(8,128)(2,1)} %cot_hbm.1, ...), custom_call_target="tpu_custom_call" | custom-call | tf_op jit(solution)/shard_map/pallas_call | solution.py:612
  44.3 2.0 %shard_map.136 = (bf16[4,256,128]{2,1,0:T(8,128)(2,1)}, bf16[4,256,128]{2,1,0:T(8,128)(2,1)}, f32[128,512]{1,0:T(8,128)}, f32[128,128]{1,0:T(8,128)}, f32[4,128]...) custom-call(bf16[4,256,128]{2,1,0:T(8,128)(2,1)} %get-tuple-element.21.refs_0_, ...), custom_call_target="tpu_custom_call" | custom-call | tf_op jit(solution)/shard_map/pallas_call | solution.py:688

commit v5 on v4

--- a/solution.py
+++ b/solution.py
@@ -181,26 +181,25 @@
     zs = [lax.rem(lax.rem(chip, 2) + o, 2) for o in range(2)]
     around = [xs[x] + zs[z] for x in (2, 1, 3, 0) for z in (1, 0)]
 
-    def row_at(n):
-        return 8 * lax.rem(y_at + 2 - n + 3 * (n // 2) - 2 * (n // 3), 4)
-
-    def each_chip(body):
+    def each_chip(body, first=0, stop=4):
         def step(n, carry):
             for offset in around:
                 body(8 * lax.rem(y_at + 2 - n + 3 * lax.div(n, 2), 4) + offset)
             return carry
 
-        lax.fori_loop(0, 3, step, 0)
-        for offset in around[:-1]:
-            body(8 * y_at + offset)
-
-    def each_peer(body):
+        lax.fori_loop(first, min(stop, 3), step, 0)
+        if stop == 4:
+            for offset in around[:-1]:
+                body(8 * y_at + offset)
+
+    def each_peer(body, first=0, stop=4):
         def both(q):
             body(2 * q + 1 - core)
             body(2 * q + core)
 
-        each_chip(both)
-        body(twin)
+        each_chip(both, first, stop)
+        if stop == 4:
+            body(twin)
 
     def near_peer(body):
         def step(t, carry):
@@ -237,9 +236,6 @@
     )
 
     rec_erc = place(rec_to_erc)
-    erc_cer = place(erc_to_cer)
-    erc_rec = place(erc_to_rec)
-    cer_erc = place(cer_to_erc)
     row_of = lax.broadcasted_iota(jnp.int32, (16, CH), 0)
     pick = jnp.where(
         (lax.broadcasted_iota(jnp.int32, (16, HEADS), 0) & 3)
@@ -248,6 +244,51 @@
         0.0,
     ).astype(BF16)
 
+    for n in (0, 2, 3, 5):
+        loads[n].wait()
+    gain = gain_ref[...]
+    shift = shift_ref[...]
+    wb16 = nn(pick, wb_ref[...])
+    wbr = [jnp.where((row_of >> 2) == r, wb16, 0.0).astype(BF16) for r in range(ROWS)]
+    bias = jnp.zeros((16, N), F32)
+    for r in range(ROWS):
+        x = x_ref[r].astype(F32)
+        mean = jnp.mean(x, -1, keepdims=True)
+        cen = x - mean
+        var = jnp.mean(cen * cen, -1, keepdims=True)
+        inv = lax.rsqrt(var + EPS)
+        normed = cen * inv
+        normed_ref[r] = normed
+        inv_ref[r] = jnp.broadcast_to(inv, (N, CH))
+        low = (normed * gain + shift).astype(BF16)
+        np_ref[r] = low
+        bias += nt(wbr[r], low)
+    bias_r[chip, core] = bias.astype(BF16)
+    for b in range(4):
+        block = jnp.concatenate([np_ref[r, 64 * b : 64 * b + 64, :] for r in range(ROWS)], 0)
+        pair_s[16 * b : 16 * b + 16] = nn(rec_erc, block).astype(BF16).reshape(16, 16, CH)
+
+    pl.semaphore_wait(barrier, group - 1)
+    each_chip(
+        lambda q: copy(
+            bias_x, bias_r.at[chip, core], bias_r.at[chip, core], 2 * q + core
+        ).start()
+    )
+    sent.append((bias_x, bias_r.at[pl.ds(0, chips - 1), 0]))
+    send(pair_x, lambda e: pair_s.at[e], pair_r)
+    pair_r[me] = pair_s[me]
+
+    for n in (1, 4, 6):
+        loads[n].wait()
+    for b in range(4):
+        block = jnp.concatenate([cot_ref[r, 64 * b : 64 * b + 64, :] for r in range(ROWS)], 0)
+        cot_s[16 * b : 16 * b + 16] = nn(rec_erc, block).astype(BF16).reshape(16, 16, CH)
+    send(cot_x, lambda e: cot_s.at[e], cot_r)
+    cot_r[me] = cot_s[me]
+
+    erc_cer = place(erc_to_cer)
+    erc_rec = place(erc_to_rec)
+    cer_erc = place(cer_to_erc)
     source = lax.broadcasted_iota(jnp.int32, (256, CH), 0)
     target = lax.broadcasted_iota(jnp.int32, (256, CH), 1)
     pick_in = jnp.where(
@@ -265,49 +306,10 @@
         ]
         for pair in (0, 1)
     ]
-
-    for load in loads:
-        load.wait()
-    gain = gain_ref[...]
-    shift = shift_ref[...]
-    wb16 = nn(pick, wb_ref[...])
-    wbr = [jnp.where((row_of >> 2) == r, wb16, 0.0).astype(BF16) for r in range(ROWS)]
-    bias = jnp.zeros((16, N), F32)
     for r in range(ROWS):
-        x = x_ref[r].astype(F32)
-        mean = jnp.mean(x, -1, keepdims=True)
-        cen = x - mean
-        var = jnp.mean(cen * cen, -1, keepdims=True)
-        inv = lax.rsqrt(var + EPS)
-        normed = cen * inv
-        normed_ref[r] = normed
-        inv_ref[r] = jnp.broadcast_to(inv, (N, CH))
-        low = (normed * gain + shift).astype(BF16)
-        np_ref[r] = low
-        high = normed.astype(BF16)
+        high = normed_ref[r].astype(BF16)
         high_ref[r] = high
-        low_ref[r] = (normed - high.astype(F32)).astype(BF16)
-        bias += nt(wbr[r], low)
-    for b in range(4):
-        block = jnp.concatenate([np_ref[r, 64 * b : 64 * b + 64, :] for r in range(ROWS)], 0)
-        pair_s[16 * b : 16 * b + 16] = nn(rec_erc, block).astype(BF16).reshape(16, 16, CH)
-    for b in range(4):
-        block = jnp.concatenate([cot_ref[r, 64 * b : 64 * b + 64, :] for r in range(ROWS)], 0)
-        cot_s[16 * b : 16 * b + 16] = nn(rec_erc, block).astype(BF16).reshape(16, 16, CH)
-    bias_r[chip, core] = bias.astype(BF16)
-    pair_r[me] = pair_s[me]
-    cot_r[me] = cot_s[me]
-
-    pl.semaphore_wait(barrier, group - 1)
-
-    each_chip(
-        lambda q: copy(
-            bias_x, bias_r.at[chip, core], bias_r.at[chip, core], 2 * q + core
-        ).start()
-    )
-    sent.append((bias_x, bias_r.at[pl.ds(0, chips - 1), 0]))
-    send(pair_x, lambda e: pair_s.at[e], pair_r)
-    send(cot_x, lambda e: cot_s.at[e], cot_r)
+        low_ref[r] = (normed_ref[r] - high.astype(F32)).astype(BF16)
 
     w_in = win_ref[...]
     w_in_t = jnp.transpose(w_in.astype(F32)).astype(BF16)
@@ -359,20 +361,12 @@
         gated_ref[j, rows, :] = (gate_ref[j, rows, :] * att).astype(BF16)
 
     wait_recv(cot_x, cot_r.at[pl.ds(0, group - 1)])
-    for j in range(COLS):
-        tmp_ref[j] = tn(gated_ref[j], w_out).astype(BF16)
-    for b in range(4):
-        block = jnp.concatenate([tmp_ref[j, 64 * b : 64 * b + 64, :] for j in range(COLS)], 0)
-        upd_s[16 * b : 16 * b + 16] = nn(cer_erc, block).astype(BF16).reshape(16, 16, CH)
+    for b in range(4):
         got = nn(erc_cer, cot_r[16 * b : 16 * b + 16].reshape(256, CH)).astype(BF16)
         for c in range(COLS):
             cotc_ref[c, 64 * b : 64 * b + 64, :] = got[64 * c : 64 * c + 64]
-    upd_r[me] = upd_s[me]
     for j in range(COLS):
         dgate_ref[j] = nt(w_out, cotc_ref[j])
-
-    def send_upd(e):
-        copy(upd_x, upd_s.at[e], upd_r.at[me], e).start()
 
     def score_grads(heads):
         for j in range(COLS):
@@ -424,42 +418,21 @@
                 0,
             )
             got = nn(cer_erc, block.astype(BF16)).astype(BF16)
-            bg_s[pair, 8 * b : 8 * b + 8] = got.reshape(8, 2, 16, CH)
-        passing = copy(bg_w + pair, bg_s.at[pair, :, 1 - core], bg_x.at[pair], twin)
-        passing.start()
-        return passing
-
-    def send_bias(pair, passing):
-        passing.wait()
-        for q in range(chips):
-            bg_t[pair, q] = (
-                bg_s[pair, q, core].astype(F32) + bg_x[pair, q].astype(F32)
-            ).astype(BF16)
-        bg_r[pair, chip] = bg_t[pair, chip]
-        each_chip(
-            lambda q: copy(
-                bg_x_ + pair, bg_t.at[pair, q], bg_r.at[pair, chip], 2 * q + core
-            ).start()
-        )
-        sent.append((bg_x_ + pair, bg_r.at[pair, pl.ds(0, chips - 1)]))
-
-    for j in range(COLS):
-        for offset in around[:-1]:
-            send_upd(2 * (row_at(j) + offset) + 1 - core)
-            send_upd(2 * (row_at(j) + offset) + core)
-    for n in range(3):
-        send_upd(2 * (row_at(n) + around[-1]) + 1 - core)
-        send_upd(2 * (row_at(n) + around[-1]) + core)
-    send_upd(twin)
-    sent.append((upd_x, upd_r.at[pl.ds(0, group - 1)]))
-
-    score_grads((0, 1))
-    first_pass = gather_bias(0)
-    score_grads((2, 3))
-    second_pass = gather_bias(1)
+            bg_s[8 * b : 8 * b + 8, :, 16 * pair : 16 * pair + 16] = got.reshape(8, 2, 16, CH)
+
+    every = tuple(range(HEADS))
+    score_grads(every)
+    gather_bias(0)
+    gather_bias(1)
+    bg_pass = copy(bg_w, bg_s.at[:, 1 - core], bg_x, twin)
+    bg_pass.start()
     input_grads((0, 1))
-    send_bias(0, first_pass)
-    send_bias(1, second_pass)
+    bg_pass.wait()
+    for q in range(chips):
+        bg_t[q] = (bg_s[q, core].astype(F32) + bg_x[q].astype(F32)).astype(BF16)
+    each_chip(lambda q: copy(bg_x_, bg_t.at[q], bg_r.at[chip], 2 * q + core).start())
+    sent.append((bg_x_, bg_r.at[pl.ds(0, chips - 1)]))
+    bg_r[chip] = bg_t[chip]
     input_grads((2, 3))
 
     g_out = nn(gated_ref[0], cotc_ref[0])
@@ -469,44 +442,58 @@
         g_in += nn(dproj_ref[j], cols_ref[j])
     par_f[pl.ds(8, group, stride=16), :] = g_out[:group]
     par_f[pl.ds(9, group, stride=16), :] = g_out[group:]
-    for j in range(COLS):
-        tmp_ref[j] = jnp.transpose(nn(w_in, dproj_ref[j])).astype(BF16)
-
-    for b in range(4):
-        block = jnp.concatenate([tmp_ref[j, 64 * b : 64 * b + 64, :] for j in range(COLS)], 0)
-        dcol_s[16 * b : 16 * b + 16] = nn(cer_erc, block).astype(BF16).reshape(16, 16, CH)
-    dcol_r[me] = dcol_s[me]
-
     for e in range(group):
         par_f[16 * e : 16 * e + 8, :] = g_in[8 * e : 8 * e + 8]
     par_s[...] = par_f[...].astype(BF16).reshape(chips, 2, 16, CH)
     par_pass = copy(par_w, par_s.at[:, 1 - core], par_x, twin)
     par_pass.start()
-    send(dcol_x, lambda e: dcol_s.at[e], dcol_r)
+
+    for j in range(COLS):
+        tmp_ref[j] = jnp.transpose(nn(w_in, dproj_ref[j])).astype(BF16)
+    for b in range(4):
+        block = jnp.concatenate([tmp_ref[j, 64 * b : 64 * b + 64, :] for j in range(COLS)], 0)
+        dcol_s[16 * b : 16 * b + 16] = nn(cer_erc, block).astype(BF16).reshape(16, 16, CH)
+
+    def send_dcol(e):
+        copy(dcol_x, dcol_s.at[e], dcol_r.at[me], e).start()
+
+    each_peer(send_dcol, 0, 2)
     par_pass.wait()
     for q in range(chips):
         par_t[q] = (par_s[q, core].astype(F32) + par_x[q].astype(F32)).astype(BF16)
-    par_r[chip] = par_t[chip]
     each_chip(lambda q: copy(par_x_, par_t.at[q], par_r.at[chip], 2 * q + core).start())
     sent.append((par_x_, par_r.at[pl.ds(0, chips - 1)]))
-
-    wait_recv(upd_x, upd_r.at[pl.ds(0, group - 1)])
-    for b in range(4):
-        got = nn(erc_rec, upd_r[16 * b : 16 * b + 16].reshape(256, CH)).astype(BF16)
-        for r in range(ROWS):
-            upd_ref[r, 64 * b : 64 * b + 64, :] = got[64 * r : 64 * r + 64]
-    stores[0].start()
-
-    wait_recv(dcol_x, dcol_r.at[pl.ds(0, group - 1)])
-    for b in range(4):
-        got = nn(erc_rec, dcol_r[16 * b : 16 * b + 16].reshape(256, CH))
-        for r in range(ROWS):
-            dn_ref[r, 64 * b : 64 * b + 64, :] = got[64 * r : 64 * r + 64]
-    grad_gain = jnp.zeros((1, CH), F32)
-    grad_shift = jnp.zeros((1, CH), F32)
+    each_peer(send_dcol, 2, 4)
+    sent.append((dcol_x, dcol_r.at[pl.ds(0, group - 1)]))
+    par_r[chip] = par_t[chip]
+    dcol_r[me] = dcol_s[me]
+
+    for j in range(COLS):
+        tmp_ref[j] = tn(gated_ref[j], w_out).astype(BF16)
+    for b in range(4):
+        block = jnp.concatenate([tmp_ref[j, 64 * b : 64 * b + 64, :] for j in range(COLS)], 0)
+        upd_s[16 * b : 16 * b + 16] = nn(cer_erc, block).astype(BF16).reshape(16, 16, CH)
+    send(upd_x, lambda e: upd_s.at[e], upd_r)
+    upd_r[me] = upd_s[me]
+
+    wait_recv(bg_x_, bg_r.at[pl.ds(0, chips - 1)])
+    sums = bg_r[0].astype(F32)
+    for s in range(1, chips):
+        sums += bg_r[s].astype(F32)
+    sums = sums.astype(BF16)
+    bsum = jnp.concatenate(
+        [nn(heads_at[0][half], sums[:16]) + nn(heads_at[1][half], sums[16:]) for half in (0, 1)],
+        1,
+    ).astype(BF16)
+    gwb = jnp.zeros((16, CH), F32)
+    part = jnp.zeros((16, CH), F32)
     for r in range(ROWS):
-        grad_gain += jnp.sum(dn_ref[r] * normed_ref[r], 0, keepdims=True)
-        grad_shift += jnp.sum(dn_ref[r], 0, keepdims=True)
+        here = (row_of >> 2) == r
+        gwb += jnp.where(here, nn(bsum, np_ref[r]), 0.0)
+        part += jnp.where(here, nn(bsum, high_ref[r]) + nn(bsum, low_ref[r]), 0.0)
+    small_s[0:4, :] = gwb[0:4] + gwb[4:8] + gwb[8:12] + gwb[12:16]
+    grad_gain = jnp.sum(part * wb16, 0, keepdims=True)
+    grad_shift = jnp.sum(jnp.sum(bsum.astype(F32), 1, keepdims=True) * wb16, 0, keepdims=True)
 
     wait_recv(par_x_, par_r.at[pl.ds(0, chips - 1)])
     total = par_r[0].astype(F32)
@@ -518,29 +505,18 @@
     )
     sent.append((sum_x, sum_r.at[pl.ds(0, chips - 1), 0]))
 
-    sums = []
-    for pair in range(2):
-        wait_recv(bg_x_ + pair, bg_r.at[pair, pl.ds(0, chips - 1)])
-        bsum = bg_r[pair, 0].astype(F32)
-        for s in range(1, chips):
-            bsum += bg_r[pair, s].astype(F32)
-        sums.append(bsum.astype(BF16))
-    bsum = jnp.concatenate(
-        [nn(heads_at[0][half], sums[0]) + nn(heads_at[1][half], sums[1]) for half in (0, 1)], 1
-    ).astype(BF16)
-    gwb = jnp.zeros((16, CH), F32)
-    part = jnp.zeros((16, CH), F32)
+    wait_recv(dcol_x, dcol_r.at[pl.ds(0, group - 1)])
+    for b in range(4):
+        got = nn(erc_rec, dcol_r[16 * b : 16 * b + 16].reshape(256, CH))
+        for r in range(ROWS):
+            dn_ref[r, 64 * b : 64 * b + 64, :] = got[64 * r : 64 * r + 64]
     for r in range(ROWS):
-        here = (row_of >> 2) == r
-        gwb += jnp.where(here, nn(bsum, np_ref[r]), 0.0)
-        part += jnp.where(here, nn(bsum, high_ref[r]) + nn(bsum, low_ref[r]), 0.0)
-    grad_gain += jnp.sum(part * wb16, 0, keepdims=True)
-    grad_shift += jnp.sum(jnp.sum(bsum.astype(F32), 1, keepdims=True) * wb16, 0, keepdims=True)
-    small_s[0:4, :] = gwb[0:4] + gwb[4:8] + gwb[8:12] + gwb[12:16]
+        grad_gain += jnp.sum(dn_ref[r] * normed_ref[r], 0, keepdims=True)
+        grad_shift += jnp.sum(dn_ref[r], 0, keepdims=True)
     small_s[4:5, :] = grad_gain
     small_s[5:6, :] = grad_shift
+    send(small_x, lambda e: small_s, small_r, near_peer)
     small_r[me] = small_s[...]
-    send(small_x, lambda e: small_s, small_r, near_peer)
 
     for r in range(ROWS):
         normed = normed_ref[r]
@@ -549,6 +525,13 @@
         mean_sn = jnp.mean(scaled * normed, -1, keepdims=True)
         gp_ref[r] = (inv_ref[r] * (scaled - mean_s - normed * mean_sn)).astype(BF16)
     stores[1].start()
+
+    wait_recv(upd_x, upd_r.at[pl.ds(0, group - 1)])
+    for b in range(4):
+        got = nn(erc_rec, upd_r[16 * b : 16 * b + 16].reshape(256, CH)).astype(BF16)
+        for r in range(ROWS):
+            upd_ref[r, 64 * b : 64 * b + 64, :] = got[64 * r : 64 * r + 64]
+    stores[0].start()
 
     wait_recv(sum_x, sum_r.at[pl.ds(0, chips - 1), 0])
     sum_pass = copy(sum_w, sum_r.at[:, core], sum_r.at[:, core], twin)
@@ -651,10 +634,10 @@
             pltpu.VMEM(block, BF16),
             pltpu.VMEM(block, BF16),
             pltpu.VMEM(block, BF16),
-            pltpu.VMEM((2, chips, 2, 16, CH), BF16),
-            pltpu.VMEM((2, chips, 16, CH), BF16),
-            pltpu.VMEM((2, chips, 16, CH), BF16),
-            pltpu.VMEM((2, chips, 16, CH), BF16),
+            pltpu.VMEM((chips, 2, 32, CH), BF16),
+            pltpu.VMEM((chips, 32, CH), BF16),
+            pltpu.VMEM((chips, 32, CH), BF16),
+            pltpu.VMEM((chips, 32, CH), BF16),
             pltpu.VMEM((COLS * HEADS, N, N), F32),
             pltpu.VMEM((COLS, CH, N), BF16),
             pltpu.VMEM((COLS, 8, N), F32),

time: 46.3 us -> 45.7 us (0.987)
  Pallas kernels: 44.9 us -> 44.3 us
    pallas_call x1, Pallas kernels: 43 us -> 42.3 us  [per_device(): pl.pallas_call(functools.partial(kernel, group), out_shape=shapes, in_spe...]
where the time goes in v5:
time: 45.7 us; the launch traced here: 45.6 us
  Pallas kernels  44.3 us (97%)
  between operations  1.29 us (3%)
    pallas_call x1, Pallas kernels, per_device(): pl.pallas_call(functools.partial(kernel, group), out_shape=shapes, in_spe...  42.3 us
    pallas_call x1, Pallas kernels, per_device(): pl.pallas_call(finish, out_shape=shapes, in_specs=[hbm] * 7, out_specs=[h...  1.97 us

profile of v5, /device:TPU:1, one launch (start us, length us, event | category | flops | bytes accessed | tf_op | source)
XLA Modules:
  0.0 45.6 jit_solution(6761877035423030029)
XLA Ops:
  1.3 42.3 %shard_map.135 = (bf16[4,256,128]{2,1,0:T(8,128)(2,1)}, bf16[4,256,128]{2,1,0:T(8,128)(2,1)}, f32[128,512]{1,0:T(8,128)}, f32[128,128]{1,0:T(8,128)}, f32[4,128]...) custom-call(bf16[4,256,128]{2,1,0:T(8,128)(2,1)} %x_hbm.1, bf16[4,256,128]{2,1,0:T(8,128)(2,1)} %cot_hbm.1, ...), custom_call_target="tpu_custom_call" | custom-call | tf_op jit(solution)/shard_map/pallas_call | solution.py:595
  43.6 2.0 %shard_map.136 = (bf16[4,256,128]{2,1,0:T(8,128)(2,1)}, bf16[4,256,128]{2,1,0:T(8,128)(2,1)}, f32[128,512]{1,0:T(8,128)}, f32[128,128]{1,0:T(8,128)}, f32[4,128]...) custom-call(bf16[4,256,128]{2,1,0:T(8,128)(2,1)} %get-tuple-element.21.refs_0_, ...), custom_call_target="tpu_custom_call" | custom-call | tf_op jit(solution)/shard_map/pallas_call | solution.py:671

commit v6 on v5

--- a/solution.py
+++ b/solution.py
@@ -201,13 +201,6 @@
         if stop == 4:
             body(twin)
 
-    def near_peer(body):
-        def step(t, carry):
-            body(lax.rem(me + t, group))
-            return carry
-
-        lax.fori_loop(1, group, step, 0)
-
     def copy(which, src, dst, device):
         return pltpu.make_async_remote_copy(
             src_ref=src,
@@ -220,8 +213,8 @@
 
     sent = []
 
-    def send(which, source_of, dest, order=each_peer):
-        order(lambda e: copy(which, source_of(e), dest.at[me], e).start())
+    def send(which, source_of, dest):
+        each_peer(lambda e: copy(which, source_of(e), dest.at[me], e).start())
         sent.append((which, dest.at[pl.ds(0, group - 1)]))
 
     def wait_recv(which, part):
@@ -231,7 +224,7 @@
         pltpu.make_async_copy(part, part, send_sem.at[which]).wait()
 
     barrier = pltpu.get_barrier_semaphore()
-    near_peer(
+    each_peer(
         lambda e: pl.semaphore_signal(barrier, inc=1, device_id={"dap": e}, device_id_type=MESH)
     )
 
@@ -392,10 +385,10 @@
                     bacc_ref[h] += ds
                 ds_ref[HEADS * j + h] = ds.astype(BF16)
 
-    def input_grads(heads):
-        for which in range(3):
+    def input_grads(kinds):
+        for which in kinds:
             for j in range(COLS):
-                for h in heads:
+                for h in range(HEADS):
                     ds = ds_ref[HEADS * j + h]
                     if which == 0:
                         grad = nn(part_of(1, j, h), ds) * scale
@@ -433,7 +426,7 @@
     each_chip(lambda q: copy(bg_x_, bg_t.at[q], bg_r.at[chip], 2 * q + core).start())
     sent.append((bg_x_, bg_r.at[pl.ds(0, chips - 1)]))
     bg_r[chip] = bg_t[chip]
-    input_grads((2, 3))
+    input_grads((2,))
 
     g_out = nn(gated_ref[0], cotc_ref[0])
     g_in = nn(dproj_ref[0], cols_ref[0])
@@ -515,7 +508,7 @@
         grad_shift += jnp.sum(dn_ref[r], 0, keepdims=True)
     small_s[4:5, :] = grad_gain
     small_s[5:6, :] = grad_shift
-    send(small_x, lambda e: small_s, small_r, near_peer)
+    send(small_x, lambda e: small_s, small_r)
     small_r[me] = small_s[...]
 
     for r in range(ROWS):

time: 45.7 us -> 46.1 us (level)
  no operation moved by 1% of the time
where the time goes in v6:
time: 46.1 us; the launch traced here: 46 us
  Pallas kernels  44.7 us (97%)
  between operations  1.29 us (3%)
    pallas_call x1, Pallas kernels, per_device(): pl.pallas_call(functools.partial(kernel, group), out_shape=shapes, in_spe...  42.8 us
    pallas_call x1, Pallas kernels, per_device(): pl.pallas_call(finish, out_shape=shapes, in_specs=[hbm] * 7, out_specs=[h...  1.97 us

profile of v6, /device:TPU:1, one launch (start us, length us, event | category | flops | bytes accessed | tf_op | source)
XLA Modules:
  0.0 46.0 jit_solution(12010926759785586410)
XLA Ops:
  1.3 42.8 %shard_map.135 = (bf16[4,256,128]{2,1,0:T(8,128)(2,1)}, bf16[4,256,128]{2,1,0:T(8,128)(2,1)}, f32[128,512]{1,0:T(8,128)}, f32[128,128]{1,0:T(8,128)}, f32[4,128]...) custom-call(bf16[4,256,128]{2,1,0:T(8,128)(2,1)} %x_hbm.1, bf16[4,256,128]{2,1,0:T(8,128)(2,1)} %cot_hbm.1, ...), custom_call_target="tpu_custom_call" | custom-call | tf_op jit(solution)/shard_map/pallas_call | solution.py:588
  44.0 2.0 %shard_map.136 = (bf16[4,256,128]{2,1,0:T(8,128)(2,1)}, bf16[4,256,128]{2,1,0:T(8,128)(2,1)}, f32[128,512]{1,0:T(8,128)}, f32[128,128]{1,0:T(8,128)}, f32[4,128]...) custom-call(bf16[4,256,128]{2,1,0:T(8,128)(2,1)} %get-tuple-element.21.refs_0_, ...), custom_call_target="tpu_custom_call" | custom-call | tf_op jit(solution)/shard_map/pallas_call | solution.py:664

commit v7 on v5

--- a/solution.py
+++ b/solution.py
@@ -68,18 +68,10 @@
     wo_hbm,
     upd_hbm,
     gp_hbm,
-    gwin_hbm,
-    gwo_hbm,
-    gwb_hbm,
-    gg_hbm,
-    gs_hbm,
+    sum_hbm,
+    small_hbm,
     upd_ref,
     gp_ref,
-    gwin_ref,
-    gwo_ref,
-    gwb_ref,
-    gg_ref,
-    gs_ref,
     x_ref,
     cot_ref,
     gain_ref,
@@ -130,7 +122,6 @@
     par_r,
     sum_r,
     small_s,
-    small_r,
     in_sem,
     out_sem,
     send_sem,
@@ -167,11 +158,8 @@
             (
                 (upd_ref, upd_hbm),
                 (gp_ref, gp_hbm),
-                (gwin_ref, gwin_hbm),
-                (gwo_ref, gwo_hbm),
-                (gwb_ref, gwb_hbm),
-                (gg_ref, gg_hbm),
-                (gs_ref, gs_hbm),
+                (sum_r, sum_hbm.at[:, core]),
+                (small_s, small_hbm.at[me]),
             )
         )
     ]
@@ -289,11 +277,6 @@
     erc_cer = place(erc_to_cer)
     erc_rec = place(erc_to_rec)
     cer_erc = place(cer_to_erc)
-    source = lax.broadcasted_iota(jnp.int32, (256, CH), 0)
-    target = lax.broadcasted_iota(jnp.int32, (256, CH), 1)
-    pick_in = jnp.where(
-        (target >> 3) * 16 + (target & 7) == source, 1.0, 0.0
-    ).astype(BF16)
     par_f[...] = jnp.zeros_like(par_f)
     row = lax.broadcasted_iota(jnp.int32, (16, 16), 0)
     col = lax.broadcasted_iota(jnp.int32, (16, 16), 1)
@@ -499,11 +482,9 @@
     total = par_r[0].astype(F32)
     for s in range(1, chips):
         total += par_r[s].astype(F32)
-    sum_r[chip, core] = total.astype(BF16)
-    each_chip(
-        lambda q: copy(sum_x, sum_r.at[chip, core], sum_r.at[chip, core], 2 * q + core).start()
-    )
-    sent.append((sum_x, sum_r.at[pl.ds(0, chips - 1), 0]))
+    sum_r[chip] = total.astype(BF16)
+    each_chip(lambda q: copy(sum_x, sum_r.at[chip], sum_r.at[chip], 2 * q + core).start())
+    sent.append((sum_x, sum_r.at[pl.ds(0, chips - 1)]))
 
     wait_recv(dcol_x, dcol_r.at[pl.ds(0, group - 1)])
     for b in range(4):
@@ -515,8 +496,8 @@
         grad_shift += jnp.sum(dn_ref[r], 0, keepdims=True)
     small_s[4:5, :] = grad_gain
     small_s[5:6, :] = grad_shift
-    send(small_x, lambda e: small_s, small_r, near_peer)
-    small_r[me] = small_s[...]
+    send(small_x, lambda e: small_s, small_hbm)
+    stores[3].start()
 
     for r in range(ROWS):
         normed = normed_ref[r]
@@ -533,46 +514,92 @@
             upd_ref[r, 64 * b : 64 * b + 64, :] = got[64 * r : 64 * r + 64]
     stores[0].start()
 
-    wait_recv(sum_x, sum_r.at[pl.ds(0, chips - 1), 0])
-    sum_pass = copy(sum_w, sum_r.at[:, core], sum_r.at[:, core], twin)
+    wait_recv(sum_x, sum_r.at[pl.ds(0, chips - 1)])
+    sum_pass = copy(sum_w, sum_r, sum_hbm.at[:, core], twin)
     sum_pass.start()
+    stores[2].start()
     sum_pass.wait()
+    wait_recv(small_x, small_hbm.at[pl.ds(0, group - 1)])
+
+    for which, part in sent:
+        wait_send(which, part)
+    for store in stores:
+        store.wait()
+
+
+def finish(
+    group,
+    upd_hbm,
+    gp_hbm,
+    sum_hbm,
+    small_hbm,
+    upd_out,
+    gp_out,
+    gwin_out,
+    gwo_out,
+    gwb_out,
+    gg_out,
+    gs_out,
+    upd_ref,
+    gp_ref,
+    sum_ref,
+    small_ref,
+    gwin_ref,
+    gwo_ref,
+    gwb_ref,
+    gg_ref,
+    gs_ref,
+    par_f,
+    in_sem,
+    out_sem,
+):
+    loads = [
+        pltpu.make_async_copy(src, dst, in_sem.at[n])
+        for n, (src, dst) in enumerate(
+            ((sum_hbm, sum_ref), (small_hbm, small_ref), (upd_hbm, upd_ref), (gp_hbm, gp_ref))
+        )
+    ]
+    stores = [
+        pltpu.make_async_copy(src, dst, out_sem.at[n])
+        for n, (src, dst) in enumerate(
+            (
+                (upd_ref, upd_out),
+                (gp_ref, gp_out),
+                (gwin_ref, gwin_out),
+                (gwo_ref, gwo_out),
+                (gwb_ref, gwb_out),
+                (gg_ref, gg_out),
+                (gs_ref, gs_out),
+            )
+        )
+    ]
+    for load in loads:
+        load.start()
+    source = lax.broadcasted_iota(jnp.int32, (256, CH), 0)
+    target = lax.broadcasted_iota(jnp.int32, (256, CH), 1)
+    pick_in = jnp.where((target >> 3) * 16 + (target & 7) == source, 1.0, 0.0).astype(BF16)
+
+    loads[0].wait()
     for q in range(4):
-        rows = sum_r[8 * q : 8 * q + 8].reshape(256, CH)
+        rows = sum_ref[8 * q : 8 * q + 8].reshape(256, CH)
         gwin_ref[:, CH * q : CH * q + CH] = tn(rows, pick_in)
     stores[2].start()
-    par_f[...] = sum_r[...].astype(F32).reshape(group * 16, CH)
+    par_f[...] = sum_ref[...].astype(F32).reshape(group * 16, CH)
     gwo_ref[0:group, :] = par_f[pl.ds(8, group, stride=16), :]
     gwo_ref[group:, :] = par_f[pl.ds(9, group, stride=16), :]
     stores[3].start()
-
-    wait_recv(small_x, small_r.at[pl.ds(0, group - 1)])
-    small = small_r[0]
+    loads[1].wait()
+    small = small_ref[0]
     for s in range(1, group):
-        small += small_r[s]
+        small += small_ref[s]
     gwb_ref[...] = small[0:HEADS]
     gg_ref[...] = small[4:5]
     gs_ref[...] = small[5:6]
     for n in (4, 5, 6):
         stores[n].start()
-
-    for which, part in sent:
-        wait_send(which, part)
-    for store in stores:
-        store.wait()
-
-
-def finish(*refs):
-    count = 7
-    sources, results, held = refs[:count], refs[count : 2 * count], refs[2 * count : 3 * count]
-    in_sem, out_sem = refs[3 * count :]
-    loads = [pltpu.make_async_copy(sources[n], held[n], in_sem.at[n]) for n in range(count)]
-    stores = [pltpu.make_async_copy(held[n], results[n], out_sem.at[n]) for n in range(count)]
-    for load in loads:
-        load.start()
-    for load, store in zip(loads, stores):
-        load.wait()
-        store.start()
+    for n in (0, 1):
+        loads[2 + n].wait()
+        stores[n].start()
     for store in stores:
         store.wait()
 
@@ -592,12 +619,16 @@
         jax.ShapeDtypeStruct((1, CH), F32),
         jax.ShapeDtypeStruct((1, CH), F32),
     )
+    passed = shapes[:2] + (
+        jax.ShapeDtypeStruct((chips, 2, 16, CH), BF16),
+        jax.ShapeDtypeStruct((group, 6, CH), F32),
+    )
     out = pl.pallas_call(
         functools.partial(kernel, group),
-        out_shape=shapes,
+        out_shape=passed,
         in_specs=[hbm, hbm, smem] + [hbm] * 5,
-        out_specs=[hbm] * 7,
-        scratch_shapes=[pltpu.VMEM(s.shape, s.dtype) for s in shapes]
+        out_specs=[hbm] * 4,
+        scratch_shapes=[pltpu.VMEM(s.shape, s.dtype) for s in shapes[:2]]
         + [
             pltpu.VMEM((ROWS, N, CH), BF16),
             pltpu.VMEM((ROWS, N, CH), BF16),
@@ -647,9 +678,8 @@
             pltpu.VMEM((chips, 16, CH), BF16),
             pltpu.VMEM((chips, 16, CH), BF16),
             pltpu.VMEM((chips, 16, CH), BF16),
-            pltpu.VMEM((chips, 2, 16, CH), BF16),
+            pltpu.VMEM((chips, 16, CH), BF16),
             pltpu.VMEM((6, CH), F32),
-            pltpu.VMEM((group, 6, CH), F32),
             pltpu.SemaphoreType.DMA((7,)),
             pltpu.SemaphoreType.DMA((7,)),
             pltpu.SemaphoreType.DMA((15,)),
@@ -669,12 +699,17 @@
         w_out,
     )
     out = pl.pallas_call(
-        finish,
+        functools.partial(finish, group),
         out_shape=shapes,
-        in_specs=[hbm] * 7,
+        in_specs=[hbm] * 4,
         out_specs=[hbm] * 7,
-        scratch_shapes=[pltpu.VMEM(s.shape, s.dtype) for s in shapes]
-        + [pltpu.SemaphoreType.DMA((7,)), pltpu.SemaphoreType.DMA((7,))],
+        scratch_shapes=[pltpu.VMEM(s.shape, s.dtype) for s in passed]
+        + [pltpu.VMEM(s.shape, s.dtype) for s in shapes[2:]]
+        + [
+            pltpu.VMEM((group * 16, CH), F32),
+            pltpu.SemaphoreType.DMA((4,)),
+            pltpu.SemaphoreType.DMA((7,)),
+        ],
         compiler_params=pltpu.CompilerParams(vmem_limit_bytes=60 * 2**20),
     )(*out)
     return (*out[:4], out[4].T, out[5].reshape(CH), out[6].reshape(CH))

time: 45.7 us -> 44.7 us (0.978)
  Pallas kernels: 44.3 us -> 43.3 us
    pallas_call x2, Pallas kernels: 44.3 us -> 43.3 us  [the longest x1 41 us: per_device(): pl.pallas_call(functools.partial(kernel, group), out_shape=passed, in_spe...]
where the time goes in v7:
time: 44.7 us; the launch traced here: 44.5 us
  Pallas kernels  43.3 us (97%)
  between operations  1.29 us (3%)
    pallas_call x1, Pallas kernels, per_device(): pl.pallas_call(functools.partial(kernel, group), out_shape=passed, in_spe...  41 us
    pallas_call x1, Pallas kernels, per_device(): pl.pallas_call(functools.partial(finish, group), out_shape=shapes, in_spe...  2.24 us

profile of v7, /device:TPU:1, one launch (start us, length us, event | category | flops | bytes accessed | tf_op | source)
XLA Modules:
  0.0 44.5 jit_solution(15272531778272475823)
XLA Ops:
  1.3 41.0 %shard_map.135 = (bf16[4,256,128]{2,1,0:T(8,128)(2,1)}, bf16[4,256,128]{2,1,0:T(8,128)(2,1)}, bf16[32,2,16,128]{3,2,1,0:T(8,128)(2,1)}, f32[64,6,128]{2,1,0:T(8,128)}) custom-call(bf16[4,256,128]{2,1,0:T(8,128)(2,1)} %x_hbm.1, bf16[4,256,128]{2,1,0:T(8,128)(2,1)} %cot_hbm.1, s32[1]{0:T(128)S(6)} %copy.15.len_ref, f32[1,128]{1,0:T(1,128)} %bitcast.7, ...), custom_call_target="tpu_custom_call" | custom-call | tf_op jit(solution)/shard_map/pallas_call | solution.py:626
  42.3 2.2 %shard_map.136 = (bf16[4,256,128]{2,1,0:T(8,128)(2,1)}, bf16[4,256,128]{2,1,0:T(8,128)(2,1)}, f32[128,512]{1,0:T(8,128)}, f32[128,128]{1,0:T(8,128)}, f32[4,128]...) custom-call(bf16[4,256,128]{2,1,0:T(8,128)(2,1)} %get-tuple-element.18.upd_hbm, ...), custom_call_target="tpu_custom_call" | custom-call | tf_op jit(solution)/shard_map/pallas_call | solution.py:701

commit v8 on v7

--- a/solution.py
+++ b/solution.py
@@ -238,10 +238,11 @@
     shift = shift_ref[...]
     wb16 = nn(pick, wb_ref[...])
     wbr = [jnp.where((row_of >> 2) == r, wb16, 0.0).astype(BF16) for r in range(ROWS)]
+    average = jnp.full((CH, CH), 1.0 / CH, BF16)
     bias = jnp.zeros((16, N), F32)
     for r in range(ROWS):
         x = x_ref[r].astype(F32)
-        mean = jnp.mean(x, -1, keepdims=True)
+        mean = nn(x_ref[r], average)
         cen = x - mean
         var = jnp.mean(cen * cen, -1, keepdims=True)
         inv = lax.rsqrt(var + EPS)
@@ -579,6 +580,9 @@
     target = lax.broadcasted_iota(jnp.int32, (256, CH), 1)
     pick_in = jnp.where((target >> 3) * 16 + (target & 7) == source, 1.0, 0.0).astype(BF16)
 
+    for n in (0, 1):
+        loads[2 + n].wait()
+        stores[n].start()
     loads[0].wait()
     for q in range(4):
         rows = sum_ref[8 * q : 8 * q + 8].reshape(256, CH)
@@ -596,9 +600,6 @@
     gg_ref[...] = small[4:5]
     gs_ref[...] = small[5:6]
     for n in (4, 5, 6):
-        stores[n].start()
-    for n in (0, 1):
-        loads[2 + n].wait()
         stores[n].start()
     for store in stores:
         store.wait()

time: 44.7 us -> 44.7 us (level)
  no operation moved by 1% of the time
where the time goes in v8:
time: 44.7 us; the launch traced here: 44.6 us
  Pallas kernels  43.3 us (97%)
  between operations  1.29 us (3%)
    pallas_call x1, Pallas kernels, per_device(): pl.pallas_call(functools.partial(kernel, group), out_shape=passed, in_spe...  41 us
    pallas_call x1, Pallas kernels, per_device(): pl.pallas_call(functools.partial(finish, group), out_shape=shapes, in_spe...  2.3 us

profile of v8, /device:TPU:1, one launch (start us, length us, event | category | flops | bytes accessed | tf_op | source)
XLA Modules:
  0.0 44.6 jit_solution(463801666652567704)
XLA Ops:
  1.3 41.0 %shard_map.135 = (bf16[4,256,128]{2,1,0:T(8,128)(2,1)}, bf16[4,256,128]{2,1,0:T(8,128)(2,1)}, bf16[32,2,16,128]{3,2,1,0:T(8,128)(2,1)}, f32[64,6,128]{2,1,0:T(8,128)}) custom-call(bf16[4,256,128]{2,1,0:T(8,128)(2,1)} %x_hbm.1, bf16[4,256,128]{2,1,0:T(8,128)(2,1)} %cot_hbm.1, s32[1]{0:T(128)S(6)} %copy.15.len_ref, f32[1,128]{1,0:T(1,128)} %bitcast.7, ...), custom_call_target="tpu_custom_call" | custom-call | tf_op jit(solution)/shard_map/pallas_call | solution.py:627
  42.3 2.3 %shard_map.136 = (bf16[4,256,128]{2,1,0:T(8,128)(2,1)}, bf16[4,256,128]{2,1,0:T(8,128)(2,1)}, f32[128,512]{1,0:T(8,128)}, f32[128,128]{1,0:T(8,128)}, f32[4,128]...) custom-call(bf16[4,256,128]{2,1,0:T(8,128)(2,1)} %get-tuple-element.18.upd_hbm, ...), custom_call_target="tpu_custom_call" | custom-call | tf_op jit(solution)/shard_map/pallas_call | solution.py:702
